TPU v7x, 128 devices: a whole 4x4x4 slice. The times are simulated.
128 devices in a mesh: gx: 8 (over y, core), gy: 16 (over z, x).
Axes of the slice: x: 4, y: 4, z: 4, core: 2. Of those that a mesh axis runs over, the one named last changes fastest.
Arguments:
- adjoint_final: float32 [19, 256, 32768], P(None, 'gx', 'gy'), may hold values from -6 to 6
- base_velocity: float32 [2, 3, 256, 32768], P(None, None, 'gx', 'gy'), may hold values from -0.25 to 0.25
- base_density: float32 [2, 256, 32768], P(None, 'gx', 'gy'), may hold values from 0.8 to 1.2
- heights: int32 [256, 512], P('gx', 'gy'), may hold values from 0 to 32, as said below
- sensor_cells: int32 [8, 16, 128], P('gx', 'gy'), may hold values from 0 to 65535
- sensor_misfit: float32 [2, 3, 8, 16, 128], P(None, None, 'gx', 'gy'), may hold values from -8 to 8
Outputs:
- adjoint_start: float32 [19, 256, 32768], P(None, 'gx', 'gy')
Inputs may be any that keep to these rules, and one draw needn't show every extreme that they name: `heights`: buildings stand on lots of 6 x 6 columns in a grid of 8 x 8 columns (streets have height 0); some lots are empty.
All inputs are finite; a program needn't handle non-finite values.
Results may differ from a plain program's by a relative error of at most 0.0003.
Values sent between devices are 32-bit elements; how exact they have to be, the bound alone decides.
No kernel may reach another device: no remote copies, remote signals or barrier semaphores. Data moves between devices by JAX's collectives and lax.ppermute only.
A program may use at most 192 MiB of HBM per device.

v0:
```python
import functools

import jax
import jax.numpy as jnp
from jax import lax
from jax.experimental import pallas as pl
from jax.experimental.pallas import tpu as pltpu
from jax.sharding import PartitionSpec as P

VELOCITIES = (
    (0, 0, 0),
    (1, 0, 0),
    (-1, 0, 0),
    (0, 1, 0),
    (0, -1, 0),
    (0, 0, 1),
    (0, 0, -1),
    (1, 1, 0),
    (-1, -1, 0),
    (1, -1, 0),
    (-1, 1, 0),
    (1, 0, 1),
    (-1, 0, -1),
    (1, 0, -1),
    (-1, 0, 1),
    (0, 1, 1),
    (0, -1, -1),
    (0, 1, -1),
    (0, -1, 1),
)
OPPOSITE = (0, 2, 1, 4, 3, 6, 5, 8, 7, 10, 9, 12, 11, 14, 13, 16, 15, 18, 17)
K = 19
ROWS, COLS, NZ = 32, 32, 64
TILES = COLS * NZ // 128
EXT = 48
BASE = 8
SENS = 128
STARTS_WIDE = (7, 15, 23, 31, 33)
STARTS_OWN = (8, 16, 24, 32)
X_SIDE = {"lo": (1, 7, 9, 11, 13), "hi": (2, 8, 10, 12, 14)}
Y_SIDE = {"lo": (3, 7, 10, 15, 17), "hi": (4, 8, 9, 16, 18)}
X_FIELDS = 32
Y_FIELDS = 7
F32 = jnp.float32
MB = 1024 * 1024
HBM = pl.BlockSpec(memory_space=pltpu.HBM)
VMEM = pl.BlockSpec(memory_space=pltpu.VMEM)


def add(a, b):
    if a is None:
        return b
    return a if b is None else a + b


def sub(a, b):
    if b is None:
        return a
    return -b if a is None else a - b


def lanes():
    return lax.broadcasted_iota(jnp.int32, (8, 128), 1)


class Geometry:
    def __init__(self):
        lane = lanes()
        level = lane % NZ
        self.low = lane < NZ
        self.level = level.astype(F32)
        up = jnp.where(level == NZ - 1, -1, level + 1).astype(F32)
        self.raised = {0: self.level, 1: up, -1: self.level - 1.0}


def half_turn(value):
    return pltpu.roll(value, NZ, 1)


def from_next(geo, here, after):
    return jnp.where(geo.low, after, here)


def from_previous(geo, here, before):
    return jnp.where(geo.low, here, before)


def pull(geo, read, tile, after, before, position, number):
    cx, cy, cz = VELOCITIES[number]
    row = position + cx
    if cy == 0:
        value = read(tile, number, row)
        return pltpu.roll(value, (128 - cz) % 128, 1) if cz else value
    if cy == 1:
        value = from_next(geo, read(tile, number, row), read(after, number, row))
    else:
        value = from_previous(geo, read(tile, number, row), read(before, number, row))
    return pltpu.roll(value, NZ - cz, 1)


def incoming(geo, read, tops, tile, after, before, position, numbers):
    out = [None] * K
    for number in numbers:
        cx, cy, cz = VELOCITIES[number]
        value = pull(geo, read, tile, after, before, position, number)
        if number:
            blocked = geo.raised[cz] < tops(cy, position + cx)
            value = jnp.where(blocked, read(tile, OPPOSITE[number], position), value)
        out[number] = value
    return out


def moments(f):
    plus = [None] * K
    minus = [None] * K
    for number in range(1, K, 2):
        plus[number] = add(f[number], f[number + 1])
        minus[number] = sub(f[number], f[number + 1])
    sxy, dxy = add(plus[7], plus[9]), sub(plus[7], plus[9])
    sxz, dxz = add(plus[11], plus[13]), sub(plus[11], plus[13])
    syz, dyz = add(plus[15], plus[17]), sub(plus[15], plus[17])
    twice = [None if plus[n] is None else plus[n] + plus[n] for n in (1, 3, 5)]
    mxx = add(twice[0], add(sxy, sxz))
    myy = add(twice[1], add(sxy, syz))
    mzz = add(twice[2], add(sxz, syz))
    total = add(add(add(twice[0], twice[1]), twice[2]), add(add(sxy, sxz), syz))
    if f[0] is not None:
        total = add(12.0 * f[0], total)

    def axis(main, first, second):
        doubled = None if minus[main] is None else minus[main] + minus[main]
        return add(doubled, add(first, second))

    jx = axis(1, add(minus[7], minus[9]), add(minus[11], minus[13]))
    jy = axis(3, sub(minus[7], minus[9]), add(minus[15], minus[17]))
    jz = axis(5, sub(minus[11], minus[13]), sub(minus[15], minus[17]))
    return total, (jx, jy, jz), (mxx, myy, mzz, dxy, dxz, dyz)


def mul(a, b):
    return None if a is None else a * b


def collide(f, u, force, numbers, fluid):
    total, (jx, jy, jz), (mxx, myy, mzz, dxy, dxz, dyz) = moments(f)
    ux, uy, uz = u
    qx = add(add(mul(mxx, ux), mul(dxy, uy)), mul(dxz, uz))
    qy = add(add(mul(dxy, ux), mul(myy, uy)), mul(dyz, uz))
    qz = add(add(mul(dxz, ux), mul(dyz, uy)), mul(mzz, uz))
    speed = ux * ux + uy * uy + uz * uz
    scalar = total * (0.05 + 0.075 * speed) - 0.225 * (ux * qx + uy * qy + uz * qz)
    scaled = 0.15 * total
    vector = []
    for axis, (j, q) in enumerate(((jx, qx), (jy, qy), (jz, qz))):
        vector.append(sub(0.15 * add(j, 3.0 * q), scaled * u[axis]))
    if force is not None:
        scalar = scalar - (ux * force[0] + uy * force[1] + uz * force[2])
        vector = [vector[axis] + force[axis] for axis in range(3)]
    out = {}
    along = {}
    for number in numbers:
        c = VELOCITIES[number]
        pair = number if number % 2 else number - 1
        if number == 0:
            value = scalar
        else:
            if pair not in along:
                first = VELOCITIES[pair]
                cv = None
                for axis in range(3):
                    if first[axis] == 1:
                        cv = add(cv, vector[axis])
                    elif first[axis] == -1:
                        cv = sub(cv, vector[axis])
                along[pair] = cv
            value = scalar + along[pair] if number == pair else scalar - along[pair]
        if f[number] is not None:
            value = value - 0.8 * f[number]
        out[number] = jnp.where(fluid, value, 0.0)
    return out


def split3(value):
    high = value.astype(jnp.bfloat16)
    rest = value - high.astype(F32)
    middle = rest.astype(jnp.bfloat16)
    low = (rest - middle.astype(F32)).astype(jnp.bfloat16)
    return high, middle, low


def sensor_rows(position, misfit):
    count = position.shape[-1]
    rows = lax.broadcasted_iota(jnp.int32, (EXT, count), 0)
    here = rows == position
    parts = []
    for axis in range(3):
        parts.extend(split3(jnp.where(here, misfit[axis], 0.0)))
    return jnp.concatenate(parts, axis=0)


def sensor_field(left, lane, tile):
    count = lane.shape[-1]
    cells = lax.broadcasted_iota(jnp.int32, (128, count), 0) + tile * 128
    right = jnp.where(cells == lane, 1.0, 0.0).astype(jnp.bfloat16)
    product = lax.dot_general(
        left, right, (((1,), (1,)), ((), ())), preferred_element_type=F32
    )
    field = []
    for axis in range(3):
        parts = [product[(3 * axis + part) * EXT : (3 * axis + part + 1) * EXT] for part in range(3)]
        field.append(parts[0] + (parts[1] + parts[2]))
    return field


def by_parity(parity, even, odd):
    pl.when(parity == 0)(even)
    pl.when(parity == 1)(odd)


def pack_x_kernel(parity_ref, adjoint, velocity, density, heights, cells, misfit, out_a, out_b,
                  rows_buf, u_buf, rho_buf, sems):
    copies = []
    for side, start in ((0, 0), (1, ROWS - 8)):
        for tile in range(TILES):
            at = pl.ds(tile * 128, 128)
            copies.append(
                pltpu.make_async_copy(adjoint.at[:, pl.ds(start, 8), at], rows_buf.at[side, tile], sems.at[side, tile])
            )
        copies.append(pltpu.make_async_copy(velocity.at[1, :, pl.ds(start, 8), :], u_buf.at[side], sems.at[side, TILES]))
        copies.append(pltpu.make_async_copy(density.at[1, pl.ds(start, 8), :], rho_buf.at[side], sems.at[side, TILES + 1]))
    for copy in copies:
        copy.start()
    for copy in copies:
        copy.wait()
    flat = rows_buf.reshape(2, TILES, K * 8, 128)

    def pack(side, out):
        slot = 0 if side == "lo" else 1
        first = 0 if side == "lo" else 7
        second = 1 if side == "lo" else 6
        for tile in range(TILES):
            at = pl.ds(tile * 128, 128)
            out[0:8, at] = flat[slot, tile, pl.ds(first, 8, stride=8), :]
            out[8:16, at] = flat[slot, tile, pl.ds(64 + first, 8, stride=8), :]
            out[16:19, at] = flat[slot, tile, pl.ds(128 + first, 3, stride=8), :]
            for index, number in enumerate(X_SIDE[side]):
                out[19 + index : 20 + index, at] = rows_buf[slot, tile, number, second : second + 1, :]
        for axis in range(3):
            out[24 + axis : 25 + axis, :] = u_buf[slot, axis, first : first + 1, :]
        out[27:28, :] = rho_buf[slot, first : first + 1, :]
        edge = 0 if side == "lo" else ROWS - 1
        inner = 1 if side == "lo" else ROWS - 2
        out[28:29, 0:COLS] = heights[edge : edge + 1, :].astype(F32)
        out[28:29, 128 : 128 + COLS] = heights[inner : inner + 1, :].astype(F32)
        out[28:29, 256:384] = cells[0].astype(F32)
        for axis in range(3):
            out[28:29, 384 + 128 * axis : 512 + 128 * axis] = misfit[1, axis, 0]

    def even():
        pack("hi", out_a)
        pack("lo", out_b)

    def odd():
        pack("lo", out_a)
        pack("hi", out_b)

    by_parity(parity_ref[0], even, odd)


def pack_x(parity, adjoint, velocity, density, heights, cells, misfit):
    shape = jax.ShapeDtypeStruct((X_FIELDS, TILES * 128), F32)
    return pl.pallas_call(
        pack_x_kernel,
        out_shape=(shape, shape),
        in_specs=[pl.BlockSpec(memory_space=pltpu.SMEM), HBM, HBM, HBM, VMEM, VMEM, VMEM],
        out_specs=(VMEM, VMEM),
        scratch_shapes=[
            pltpu.VMEM((2, TILES, K, 8, 128), F32),
            pltpu.VMEM((2, 3, 8, TILES * 128), F32),
            pltpu.VMEM((2, 8, TILES * 128), F32),
            pltpu.SemaphoreType.DMA((2, TILES + 2)),
        ],
        compiler_params=pltpu.CompilerParams(vmem_limit_bytes=16 * MB),
        name="pack_x",
    )(parity, adjoint, velocity, density, heights, cells, misfit)


def place_x(message, side, tiles, field, u, rho, tall):
    outer, inner = (BASE + ROWS, BASE + ROWS + 1) if side == "lo" else (BASE - 1, BASE - 2)
    flat = field.reshape(field.shape[0], K * EXT, 128)
    for slot, tile in tiles:
        at = pl.ds(tile * 128, 128)
        flat[slot, pl.ds(outer, 8, stride=EXT), :] = message[0:8, at]
        flat[slot, pl.ds(8 * EXT + outer, 8, stride=EXT), :] = message[8:16, at]
        flat[slot, pl.ds(16 * EXT + outer, 3, stride=EXT), :] = message[16:19, at]
        for index, number in enumerate(X_SIDE[side]):
            field[slot, number, inner : inner + 1, :] = message[19 + index : 20 + index, at]
        for axis in range(3):
            u[slot, axis, outer : outer + 1, :] = message[24 + axis : 25 + axis, at]
        rho[slot, outer : outer + 1, :] = message[27:28, at]
    tall[outer : outer + 1, 0:COLS] = message[28:29, 0:COLS]
    tall[inner : inner + 1, 0:COLS] = message[28:29, 128 : 128 + COLS]


def column_tops(geo, tall, tile):
    low = lax.broadcasted_iota(jnp.int32, (EXT, 128), 1) < NZ
    left = jnp.broadcast_to(tall[:, 2 * tile : 2 * tile + 1], (EXT, 128))
    right = jnp.broadcast_to(tall[:, 2 * tile + 1 : 2 * tile + 2], (EXT, 128))
    return jnp.where(low, left, right)


def own_sensors(cells, misfit, step):
    numbers = cells[0]
    return (
        numbers // (COLS * NZ) + BASE,
        numbers % (COLS * NZ),
        [misfit[step, axis, 0] for axis in range(3)],
    )


def message_sensors(message, side):
    numbers = message[28:29, 256:384].astype(jnp.int32)
    row = numbers // (COLS * NZ)
    if side == "lo":
        position = jnp.where(row == 0, BASE + ROWS, -1)
    else:
        position = jnp.where(row == ROWS - 1, BASE - 1, -1)
    return (
        position,
        numbers % (COLS * NZ),
        [message[28:29, 384 + 128 * axis : 512 + 128 * axis] for axis in range(3)],
    )


def join_sensors(parts):
    position = jnp.concatenate([part[0] for part in parts], axis=1)
    lane = jnp.concatenate([part[1] for part in parts], axis=1)
    misfit = [jnp.concatenate([part[2][axis] for part in parts], axis=1) for axis in range(3)]
    return position, lane, misfit


def pack_y_kernel(parity_ref, adjoint, velocity, density, heights, cells, misfit, msg_a, msg_b,
                  out_a, out_b, field, u, rho, tall, tops, force, partial, sems):
    slots = ((0, 0), (1, TILES - 1))
    copies = []
    for slot, tile in slots:
        at = pl.ds(tile * 128, 128)
        own = pl.ds(BASE, ROWS)
        copies.append(pltpu.make_async_copy(adjoint.at[:, :, at], field.at[slot, :, own, :], sems.at[slot, 0]))
        copies.append(pltpu.make_async_copy(velocity.at[1, :, :, at], u.at[slot, :, own, :], sems.at[slot, 1]))
        copies.append(pltpu.make_async_copy(density.at[1, :, at], rho.at[slot, own, :], sems.at[slot, 2]))
    for copy in copies:
        copy.start()
    tall[BASE : BASE + ROWS, 0:COLS] = heights[...].astype(F32)
    for copy in copies:
        copy.wait()
    geo = Geometry()
    x_parity = parity_ref[0]

    def from_x(low_msg, high_msg):
        place_x(low_msg, "lo", slots, field, u, rho, tall)
        place_x(high_msg, "hi", slots, field, u, rho, tall)
        position, lane, value = join_sensors(
            [own_sensors(cells, misfit, 1), message_sensors(low_msg, "lo"), message_sensors(high_msg, "hi")]
        )
        left = sensor_rows(position, value)
        for slot, tile in slots:
            for axis, part in enumerate(sensor_field(left, lane, tile)):
                force[slot, axis] = part

    by_parity(x_parity, lambda: from_x(msg_a, msg_b), lambda: from_x(msg_b, msg_a))
    for slot, tile in slots:
        tops[slot, 0] = column_tops(geo, tall, tile)
        for row in range(0, EXT, 8):
            tops[slot, 1, row : row + 8] = half_turn(tops[slot, 0, row : row + 8])

    def read(tile, number, row):
        return field[tile, number, pl.ds(row, 8), :]

    for slot, side in ((0, "lo"), (1, "hi")):
        inward = 1 if side == "lo" else -1
        numbers = [n for n in range(K) if VELOCITIES[n][1] in (0, inward)]
        for start in STARTS_WIDE:
            at = pl.ds(start, 8)

            def top(cy, row, slot=slot):
                return tops[slot, 0 if cy == 0 else 1, pl.ds(row, 8), :]

            f = incoming(geo, read, top, slot, slot, slot, start, numbers)
            inverse = 1.0 / rho[slot, at, :]
            velocity_here = [u[slot, axis, at, :] for axis in range(3)]
            push = [force[slot, axis, at, :] * inverse for axis in range(3)]
            fluid = geo.level >= tops[slot, 0, at, :]
            result = collide(f, velocity_here, push, Y_SIDE[side], fluid)
            for index, number in enumerate(Y_SIDE[side]):
                partial[slot, index, at, :] = result[number]

    def write(side, out):
        slot = 0 if side == "lo" else 1
        for start in range(0, 40, 8):
            at = pl.ds(start + BASE - 2, 8)
            pairs = [
                (field[slot, number, at, :], partial[slot, index, at, :])
                for index, number in enumerate(Y_SIDE[side])
            ]
            pairs.append((u[slot, 0, at, :], u[slot, 1, at, :]))
            pairs.append((u[slot, 2, at, :], tops[slot, 0, at, :]))
            for index, (first, second) in enumerate(pairs):
                turned = half_turn(second)
                if side == "lo":
                    value = jnp.where(geo.low, first, turned)
                else:
                    value = jnp.where(geo.low, turned, first)
                out[index, start : start + 8, :] = value

    def even():
        write("hi", out_a)
        write("lo", out_b)

    def odd():
        write("lo", out_a)
        write("hi", out_b)

    by_parity(parity_ref[1], even, odd)


def pack_y(parity, adjoint, velocity, density, heights, cells, misfit, msg_a, msg_b):
    shape = jax.ShapeDtypeStruct((Y_FIELDS, 40, 128), F32)
    return pl.pallas_call(
        pack_y_kernel,
        out_shape=(shape, shape),
        in_specs=[pl.BlockSpec(memory_space=pltpu.SMEM), HBM, HBM, HBM] + [VMEM] * 5,
        out_specs=(VMEM, VMEM),
        scratch_shapes=[
            pltpu.VMEM((2, K, EXT, 128), F32),
            pltpu.VMEM((2, 3, EXT, 128), F32),
            pltpu.VMEM((2, EXT, 128), F32),
            pltpu.VMEM((EXT, 128), F32),
            pltpu.VMEM((2, 2, EXT, 128), F32),
            pltpu.VMEM((2, 3, EXT, 128), F32),
            pltpu.VMEM((2, 5, EXT, 128), F32),
            pltpu.SemaphoreType.DMA((2, 3)),
        ],
        compiler_params=pltpu.CompilerParams(vmem_limit_bytes=16 * MB),
        name="pack_y",
    )(parity, adjoint, velocity, density, heights, cells, misfit, msg_a, msg_b)


def steps_kernel(parity_ref, adjoint, velocity, density, heights, cells, misfit, xmsg_a, xmsg_b, ymsg_a, ymsg_b,
                 out, field, middle, u1, u0, rho1, rho0, tall, tops, force1, force0, side_partial, side_u,
                 in_sems, out_sems):
    own = pl.ds(BASE, ROWS)

    def fetch(tile):
        at = pl.ds(pl.multiple_of(tile * 128, 128), 128)
        return [
            pltpu.make_async_copy(adjoint.at[:, :, at], field.at[tile, :, own, :], in_sems.at[tile, 0]),
            pltpu.make_async_copy(velocity.at[1, :, :, at], u1.at[tile, :, own, :], in_sems.at[tile, 1]),
            pltpu.make_async_copy(velocity.at[0, :, :, at], u0.at[tile, :, own, :], in_sems.at[tile, 2]),
            pltpu.make_async_copy(density.at[1, :, at], rho1.at[tile, own, :], in_sems.at[tile, 3]),
            pltpu.make_async_copy(density.at[0, :, at], rho0.at[tile, own, :], in_sems.at[tile, 4]),
        ]

    def start(tile, carry):
        for copy in fetch(tile):
            copy.start()
        return carry

    def arrived(tile, carry):
        for copy in fetch(tile):
            copy.wait()
        return carry

    lax.fori_loop(0, TILES, start, 0)
    geo = Geometry()
    tall[BASE : BASE + ROWS, 0:COLS] = heights[...].astype(F32)

    position, lane0, value = own_sensors(cells, misfit, 0)
    left0 = sensor_rows(position, value)

    def forces0(tile, carry):
        for axis, part in enumerate(sensor_field(left0, lane0, tile)):
            force0[tile, axis] = part
        return carry

    lax.fori_loop(0, TILES, forces0, 0)
    lax.fori_loop(0, TILES, arrived, 0)

    def from_x(low_msg, high_msg):
        slots = [(tile, tile) for tile in range(TILES)]
        place_x(low_msg, "lo", slots, field, u1, rho1, tall)
        place_x(high_msg, "hi", slots, field, u1, rho1, tall)
        position, lane1, value = join_sensors(
            [own_sensors(cells, misfit, 1), message_sensors(low_msg, "lo"), message_sensors(high_msg, "hi")]
        )
        left1 = sensor_rows(position, value)

        def forces1(tile, carry):
            for axis, part in enumerate(sensor_field(left1, lane1, tile)):
                force1[tile, axis] = part
            return carry

        lax.fori_loop(0, TILES, forces1, 0)

    by_parity(parity_ref[0], lambda: from_x(xmsg_a, xmsg_b), lambda: from_x(xmsg_b, xmsg_a))

    def from_y(low_msg, high_msg):
        for start in range(0, 40, 8):
            at = pl.ds(start + BASE - 2, 8)
            for index in range(Y_FIELDS):
                low_value = low_msg[index, start : start + 8, :]
                high_value = high_msg[index, start : start + 8, :]
                low_turned, high_turned = half_turn(low_value), half_turn(high_value)
                if index < 5:
                    field[TILES, Y_SIDE["lo"][index], at, :] = low_value
                    field[TILES, Y_SIDE["hi"][index], at, :] = high_value
                    side_partial[0, index, at, :] = low_turned
                    side_partial[1, index, at, :] = high_turned
                else:
                    first = jnp.where(geo.low, low_value, high_value)
                    second = jnp.where(geo.low, low_turned, high_turned)
                    if index == 5:
                        side_u[0, at, :] = first
                        side_u[1, at, :] = second
                    else:
                        side_u[2, at, :] = first
                        tops[0, TILES, at, :] = second

    by_parity(parity_ref[1], lambda: from_y(ymsg_a, ymsg_b), lambda: from_y(ymsg_b, ymsg_a))

    for tile in range(TILES):
        tops[0, tile] = column_tops(geo, tall, tile)
    for tile in range(TILES + 1):
        after, before = (tile + 1) % (TILES + 1), (tile - 1) % (TILES + 1)
        for row in range(0, EXT, 8):
            at = pl.ds(row, 8)
            here = tops[0, tile, at, :]
            tops[1, tile, at, :] = half_turn(from_next(geo, here, tops[0, after, at, :]))
            tops[2, tile, at, :] = half_turn(from_previous(geo, here, tops[0, before, at, :]))

    def step(source, target, u, rho, force, starts, tile):
        after = tile + 1
        before = jnp.where(tile == 0, TILES, tile - 1)

        def read(where, number, row):
            return source[where, number, pl.ds(row, 8), :]

        def top(cy, row):
            return tops[cy % 3, tile, pl.ds(row, 8), :]

        for start in starts:
            at = pl.ds(start, 8)
            f = incoming(geo, read, top, tile, after, before, start, range(K))
            inverse = 1.0 / rho[tile, at, :]
            velocity_here = [u[tile, axis, at, :] for axis in range(3)]
            push = [force[tile, axis, at, :] * inverse for axis in range(3)]
            fluid = geo.level >= tops[0, tile, at, :]
            result = collide(f, velocity_here, push, range(K), fluid)
            for number in range(K):
                target[tile, number, at, :] = result[number]

    def first_step(tile, carry):
        step(field, middle, u1, rho1, force1, STARTS_WIDE, tile)
        return carry

    lax.fori_loop(0, TILES, first_step, 0)

    def read_first(where, number, row):
        return field[where, number, pl.ds(row, 8), :]

    for slot, side, other in ((0, "lo", "hi"), (1, "hi", "lo")):
        for start in STARTS_WIDE:
            at = pl.ds(start, 8)

            def top(cy, row):
                return tops[cy % 3, TILES, pl.ds(row, 8), :]

            f = incoming(geo, read_first, top, TILES, 0, TILES - 1, start, Y_SIDE[other])
            velocity_here = [side_u[axis, at, :] for axis in range(3)]
            fluid = geo.level >= tops[0, TILES, at, :]
            result = collide(f, velocity_here, None, Y_SIDE[side], fluid)
            for index, number in enumerate(Y_SIDE[side]):
                middle[TILES, number, at, :] = result[number] + side_partial[slot, index, at, :]

    def send_out(tile):
        at = pl.ds(pl.multiple_of(tile * 128, 128), 128)
        return pltpu.make_async_copy(field.at[tile, :, own, :], out.at[:, :, at], out_sems.at[tile])

    def second_step(tile, carry):
        step(middle, field, u0, rho0, force0, STARTS_OWN, tile)
        send_out(tile).start()
        return carry

    lax.fori_loop(0, TILES, second_step, 0)

    def sent(tile, carry):
        send_out(tile).wait()
        return carry

    lax.fori_loop(0, TILES, sent, 0)


def both_steps(parity, adjoint, velocity, density, heights, cells, misfit, xmsg_a, xmsg_b, ymsg_a, ymsg_b):
    wide = TILES + 1
    return pl.pallas_call(
        steps_kernel,
        out_shape=jax.ShapeDtypeStruct(adjoint.shape, F32),
        in_specs=[pl.BlockSpec(memory_space=pltpu.SMEM), HBM, HBM, HBM] + [VMEM] * 7,
        out_specs=HBM,
        scratch_shapes=[
            pltpu.VMEM((wide, K, EXT, 128), F32),
            pltpu.VMEM((wide, K, EXT, 128), F32),
            pltpu.VMEM((TILES, 3, EXT, 128), F32),
            pltpu.VMEM((TILES, 3, EXT, 128), F32),
            pltpu.VMEM((TILES, EXT, 128), F32),
            pltpu.VMEM((TILES, EXT, 128), F32),
            pltpu.VMEM((EXT, 128), F32),
            pltpu.VMEM((3, wide, EXT, 128), F32),
            pltpu.VMEM((TILES, 3, EXT, 128), F32),
            pltpu.VMEM((TILES, 3, EXT, 128), F32),
            pltpu.VMEM((2, 5, EXT, 128), F32),
            pltpu.VMEM((3, EXT, 128), F32),
            pltpu.SemaphoreType.DMA((TILES, 5)),
            pltpu.SemaphoreType.DMA((TILES,)),
        ],
        compiler_params=pltpu.CompilerParams(vmem_limit_bytes=48 * MB),
        name="both_steps",
    )(parity, adjoint, velocity, density, heights, cells, misfit, xmsg_a, xmsg_b, ymsg_a, ymsg_b)


def partners(count, odd):
    if not odd:
        return [(i, i ^ 1) for i in range(count)]
    return [(i, (i - 1) % count if i % 2 == 0 else (i + 1) % count) for i in range(count)]


def swap(value, axis, odd):
    return lax.ppermute(value, axis, partners(lax.axis_size(axis), odd))


def per_device(adjoint, velocity, density, heights, cells, misfit):
    parity = jnp.stack([lax.axis_index("gx") % 2, lax.axis_index("gy") % 2]).astype(jnp.int32)
    args = (parity, adjoint, velocity, density, heights, cells, misfit)
    x_a, x_b = pack_x(*args)
    x_a, x_b = swap(x_a, "gx", False), swap(x_b, "gx", True)
    y_a, y_b = pack_y(*args, x_a, x_b)
    y_a, y_b = swap(y_a, "gy", False), swap(y_b, "gy", True)
    return both_steps(*args, x_a, x_b, y_a, y_b)


def solution(mesh):
    return jax.shard_map(
        per_device,
        mesh=mesh,
        in_specs=(
            P(None, "gx", "gy"),
            P(None, None, "gx", "gy"),
            P(None, "gx", "gy"),
            P("gx", "gy"),
            P("gx", "gy", None),
            P(None, None, "gx", "gy", None),
        ),
        out_specs=P(None, "gx", "gy"),
        check_vma=False,
    )
```

profile of v0, /device:TPU:0, one launch (start us, length us, event | category | flops | bytes accessed | tf_op | source)
XLA Modules:
  0.0 47.6 jit_solution(8773266365518607149)
XLA Ops:
  0.0 0.1 pad_add_fusion.parity_ref
  0.1 0.0 copy-start
  0.1 2.4 %copy-done = f32[19,32,2048]{2,1,0:T(8,128)S(1)} copy-done((f32[19,32,2048]{2,1,0:T(8,128)S(1)}, f32[19,32,2048]{2,1,0:T(8,128)}, u32[]{:S(2)}) %copy-start) | copy-done | bytes 4980760
  2.5 1.4 %copy-done.1 = f32[2,3,32,2048]{3,2,1,0:T(8,128)S(1)} copy-done((f32[2,3,32,2048]{3,2,1,0:T(8,128)S(1)}, f32[2,3,32,2048]{3,2,1,0:T(8,128)}, u32[]{:S(2)}) %copy-start.1) | copy-done | bytes 1572888
  3.9 0.0 copy-start.3
  3.9 1.0 %copy-done.3 = f32[2,32,2048]{2,1,0:T(8,128)S(1)} copy-done((f32[2,32,2048]{2,1,0:T(8,128)S(1)}, f32[2,32,2048]{2,1,0:T(8,128)}, u32[]{:S(2)}) %copy-start.3) | copy-done | bytes 524312
  4.9 0.0 copy-start.5
  4.9 0.7 %copy-done.5 = s32[32,32]{1,0:T(8,128)S(1)} copy-done((s32[32,32]{1,0:T(8,128)S(1)}, s32[32,32]{1,0:T(8,128)}, u32[]{:S(2)}) %copy-start.5) | copy-done | bytes 4120
  5.7 0.0 copy-start.7
  5.7 0.7 %copy-done.7 = f32[2,3,1,1,128]{4,3,2,1,0:T(1,128)S(1)} copy-done((f32[2,3,1,1,128]{4,3,2,1,0:T(1,128)S(1)}, f32[2,3,1,1,128]{4,3,2,1,0:T(1,128)}, u32[]{:S(2)}) %copy-start.7) | copy-done | bytes 3096
  6.3 0.7 %copy-done.9 = s32[1,1,128]{2,1,0:T(1,128)S(1)} copy-done((s32[1,1,128]{2,1,0:T(1,128)S(1)}, s32[1,1,128]{2,1,0:T(1,128)}, u32[]{:S(2)}) %copy-start.9) | copy-done | bytes 536
  7.0 1.8 %pack_x.1 = (f32[32,2048]{1,0:T(8,128)S(1)}, f32[32,2048]{1,0:T(8,128)S(1)}) custom-call(s32[2]{0:T(128)S(1)} %pad_add_fusion.parity_ref, f32[19,32,2048]{2,1,0:T(8,128)S(1)} %copy-done, f32[2,3,32,2048]{3,2,1,0:T(8,128)S(1)} %copy-done.1, f32[2,32,2048]{2,1,0:T(8,128)S(1)} %copy-done.3, s32[32,32]{1,0:T(8,128)S(1)} %copy-done.5, ...), custom_call_target="tpu_custom_call" | custom-call | tf_op jit(solution)/shard_map/pack_x/pallas_call | solution.py:272
  8.8 0.0 copy-start.2
  8.8 0.0 copy-start.4
  8.8 0.0 copy-start.6
  8.8 0.0 copy-start.8
  8.8 0.0 copy-start.10
  8.8 0.1 collective-permute-start
  8.9 3.2 %collective-permute-start.1 = (f32[32,2048]{1,0:T(8,128)S(1)}, f32[32,2048]{1,0:T(8,128)S(1)}, u32[]{:S(2)}, u32[]{:S(2)}) collective-permute-start(f32[32,2048]{1,0:T(8,128)S(1)} %get-tuple-element.10), channel_id=1, source_target_pairs={{0,112},{16,32},{32,16},{48,64},{64,48},{80,96},{96,80},{112,0},{1... | collective-permute-start | bytes 786440 | tf_op jit(solution)/shard_map/ppermute | solution.py:638
  12.1 0.0 collective-permute-done.msg_a.xmsg_a
  12.1 4.1 %collective-permute-done.1.msg_b.xmsg_b = f32[32,2048]{1,0:T(8,128)S(1)} collective-permute-done((f32[32,2048]{1,0:T(8,128)S(1)}, f32[32,2048]{1,0:T(8,128)S(1)}, u32[]{:S(2)}, u32[]{:S(2)}) %collective-permute-start.1) | collective-permute-done | bytes 262176 | tf_op jit(solution)/shard_map/ppermute | solution.py:638
  16.2 1.6 %pack_y.1 = (f32[7,40,128]{2,1,0:T(8,128)S(1)}, f32[7,40,128]{2,1,0:T(8,128)S(1)}) custom-call(s32[2]{0:T(128)S(1)} %pad_add_fusion.parity_ref, f32[19,32,2048]{2,1,0:T(8,128)S(1)} %copy-done, f32[2,3,32,2048]{3,2,1,0:T(8,128)S(1)} %copy-done.1, f32[2,32,2048]{2,1,0:T(8,128)S(1)} %copy-done.3, s32[32,32]{1,0:T(8,128)S(1)} %copy-done.5, ...), custom_call_target="tpu_custom_call" | custom-call | tf_op jit(solution)/shard_map/pack_y/pallas_call | solution.py:429
  17.8 1.6 %collective-permute-start.2 = (f32[7,40,128]{2,1,0:T(8,128)S(1)}, f32[7,40,128]{2,1,0:T(8,128)S(1)}, u32[]{:S(2)}, u32[]{:S(2)}) collective-permute-start(f32[7,40,128]{2,1,0:T(8,128)S(1)} %get-tuple-element.11), channel_id=1, source_target_pairs={{0,1},{1,0},{2,3},{3,2},{4,5},{5,4},{6,7},{7,6},{8,9},{9,8},{10,11... | collective-permute-start | bytes 430088 | tf_op jit(solution)/shard_map/ppermute | solution.py:638
  19.4 5.6 %collective-permute-start.3 = (f32[7,40,128]{2,1,0:T(8,128)S(1)}, f32[7,40,128]{2,1,0:T(8,128)S(1)}, u32[]{:S(2)}, u32[]{:S(2)}) collective-permute-start(f32[7,40,128]{2,1,0:T(8,128)S(1)} %get-tuple-element.12), channel_id=1, source_target_pairs={{0,15},{1,2},{2,1},{3,4},{4,3},{5,6},{6,5},{7,8},{8,7},{9,10},{10,... | collective-permute-start | bytes 430088 | tf_op jit(solution)/shard_map/ppermute | solution.py:638
  25.0 0.0 collective-permute-done.2.ymsg_a
  25.0 3.1 %collective-permute-done.3.ymsg_b = f32[7,40,128]{2,1,0:T(8,128)S(1)} collective-permute-done((f32[7,40,128]{2,1,0:T(8,128)S(1)}, f32[7,40,128]{2,1,0:T(8,128)S(1)}, u32[]{:S(2)}, u32[]{:S(2)}) %collective-permute-start.3) | collective-permute-done | bytes 143392 | tf_op jit(solution)/shard_map/ppermute | solution.py:638
  28.0 0.0 copy-done.2
  28.0 0.0 copy-done.4
  28.0 0.0 copy-done.6
  28.1 0.0 copy-done.8
  28.1 0.0 copy-done.10
  28.1 19.5 %both_steps.1 = f32[19,32,2048]{2,1,0:T(8,128)} custom-call(s32[2]{0:T(128)S(1)} %pad_add_fusion.parity_ref, f32[19,32,2048]{2,1,0:T(8,128)} %adjoint.5, f32[2,3,32,2048]{3,2,1,0:T(8,128)S(1)} %copy-done.2, f32[2,32,2048]{2,1,0:T(8,128)S(1)} %copy-done.4, s32[32,32]{1,0:T(8,128)S(1)} %copy-done.6, s32[1,1,128]{2,1,0:T(1,128)S(1)} %copy-done.10, ...), custom_call_target="tpu_custom_call" | custom-call | tf_op jit(solution)/shard_map/both_steps/pallas_call | solution.py:605
  (2 shorter events, 0.0 us)
Async XLA Ops:
  0.1 2.4 %copy-start = (f32[19,32,2048]{2,1,0:T(8,128)S(1)}, f32[19,32,2048]{2,1,0:T(8,128)}, u32[]{:S(2)}) copy-start(f32[19,32,2048]{2,1,0:T(8,128)} %adjoint.5) | copy-start | bytes 14942212
  2.5 1.4 %copy-start.1 = (f32[2,3,32,2048]{3,2,1,0:T(8,128)S(1)}, f32[2,3,32,2048]{3,2,1,0:T(8,128)}, u32[]{:S(2)}) copy-start(f32[2,3,32,2048]{3,2,1,0:T(8,128)} %velocity.5) | copy-start | bytes 4718596
  3.9 1.0 %copy-start.3 = (f32[2,32,2048]{2,1,0:T(8,128)S(1)}, f32[2,32,2048]{2,1,0:T(8,128)}, u32[]{:S(2)}) copy-start(f32[2,32,2048]{2,1,0:T(8,128)} %density.5) | copy-start | bytes 1572868
  4.9 0.7 %copy-start.5 = (s32[32,32]{1,0:T(8,128)S(1)}, s32[32,32]{1,0:T(8,128)}, u32[]{:S(2)}) copy-start(s32[32,32]{1,0:T(8,128)} %heights.5) | copy-start | bytes 12292
  5.7 0.7 %copy-start.7 = (f32[2,3,1,1,128]{4,3,2,1,0:T(1,128)S(1)}, f32[2,3,1,1,128]{4,3,2,1,0:T(1,128)}, u32[]{:S(2)}) copy-start(f32[2,3,1,1,128]{4,3,2,1,0:T(1,128)} %misfit.5) | copy-start | bytes 9220
  6.3 0.7 %copy-start.9 = (s32[1,1,128]{2,1,0:T(1,128)S(1)}, s32[1,1,128]{2,1,0:T(1,128)}, u32[]{:S(2)}) copy-start(s32[1,1,128]{2,1,0:T(1,128)} %cells.5) | copy-start | bytes 1540
  8.8 19.3 %copy-start.2 = (f32[2,3,32,2048]{3,2,1,0:T(8,128)S(1)}, f32[2,3,32,2048]{3,2,1,0:T(8,128)}, u32[]{:S(2)}) copy-start(f32[2,3,32,2048]{3,2,1,0:T(8,128)} %velocity.5) | copy-start | bytes 4718596
  8.8 19.3 %copy-start.4 = (f32[2,32,2048]{2,1,0:T(8,128)S(1)}, f32[2,32,2048]{2,1,0:T(8,128)}, u32[]{:S(2)}) copy-start(f32[2,32,2048]{2,1,0:T(8,128)} %density.5) | copy-start | bytes 1572868
  8.8 19.2 %copy-start.6 = (s32[32,32]{1,0:T(8,128)S(1)}, s32[32,32]{1,0:T(8,128)}, u32[]{:S(2)}) copy-start(s32[32,32]{1,0:T(8,128)} %heights.5) | copy-start | bytes 12292
  8.8 19.2 %copy-start.8 = (f32[2,3,1,1,128]{4,3,2,1,0:T(1,128)S(1)}, f32[2,3,1,1,128]{4,3,2,1,0:T(1,128)}, u32[]{:S(2)}) copy-start(f32[2,3,1,1,128]{4,3,2,1,0:T(1,128)} %misfit.5) | copy-start | bytes 9220
  8.8 19.2 %copy-start.10 = (s32[1,1,128]{2,1,0:T(1,128)S(1)}, s32[1,1,128]{2,1,0:T(1,128)}, u32[]{:S(2)}) copy-start(s32[1,1,128]{2,1,0:T(1,128)} %cells.5) | copy-start | bytes 1540
  8.8 3.3 %collective-permute-start = (f32[32,2048]{1,0:T(8,128)S(1)}, f32[32,2048]{1,0:T(8,128)S(1)}, u32[]{:S(2)}, u32[]{:S(2)}) collective-permute-start(f32[32,2048]{1,0:T(8,128)S(1)} %get-tuple-element.9), channel_id=1, source_target_pairs={{0,16},{16,0},{32,48},{48,32},{64,80},{80,64},{96,112},{112,96},{1... | collective-permute-start | bytes 786440 | tf_op jit(solution)/shard_map/ppermute | solution.py:638
  8.9 7.3 %collective-permute-start.1 = (f32[32,2048]{1,0:T(8,128)S(1)}, f32[32,2048]{1,0:T(8,128)S(1)}, u32[]{:S(2)}, u32[]{:S(2)}) collective-permute-start(f32[32,2048]{1,0:T(8,128)S(1)} %get-tuple-element.10), channel_id=1, source_target_pairs={{0,112},{16,32},{32,16},{48,64},{64,48},{80,96},{96,80},{112,0},{1... | collective-permute-start | bytes 786440 | tf_op jit(solution)/shard_map/ppermute | solution.py:638
  17.8 7.1 %collective-permute-start.2 = (f32[7,40,128]{2,1,0:T(8,128)S(1)}, f32[7,40,128]{2,1,0:T(8,128)S(1)}, u32[]{:S(2)}, u32[]{:S(2)}) collective-permute-start(f32[7,40,128]{2,1,0:T(8,128)S(1)} %get-tuple-element.11), channel_id=1, source_target_pairs={{0,1},{1,0},{2,3},{3,2},{4,5},{5,4},{6,7},{7,6},{8,9},{9,8},{10,11... | collective-permute-start | bytes 430088 | tf_op jit(solution)/shard_map/ppermute | solution.py:638
  19.4 8.6 %collective-permute-start.3 = (f32[7,40,128]{2,1,0:T(8,128)S(1)}, f32[7,40,128]{2,1,0:T(8,128)S(1)}, u32[]{:S(2)}, u32[]{:S(2)}) collective-permute-start(f32[7,40,128]{2,1,0:T(8,128)S(1)} %get-tuple-element.12), channel_id=1, source_target_pairs={{0,15},{1,2},{2,1},{3,4},{4,3},{5,6},{6,5},{7,8},{8,7},{9,10},{10,... | collective-permute-start | bytes 430088 | tf_op jit(solution)/shard_map/ppermute | solution.py:638
where the time goes:
time: 48 us; the launch traced here: 47.6 us
  Pallas kernels  22.9 us (48%)
  starting transfers between devices  10.4 us (22%)
  waiting for transfers between devices  7.13 us (15%)
  local copies, waits for them, and re-layouts  6.95 us (14%)
    pallas_call x1, Pallas kernels, both_steps(): pl.pallas_call(steps_kernel, out_shape=jax.ShapeDtypeStruct(adjoint.shape...  19.5 us
    ppermute x4, starting transfers between devices, swap(): return lax.ppermute(value, axis, partners(lax.axis_size(axis), odd))  10.4 us
    ppermute x4, waiting for transfers between devices, swap(): return lax.ppermute(value, axis, partners(lax.axis_size(axis), odd))  7.13 us
    unnamed x22, local copies, waits for them, and re-layouts  6.95 us
    pallas_call x1, Pallas kernels, pack_x(): pl.pallas_call(pack_x_kernel, out_shape=(shape, shape), in_specs=[pl.Bloc...  1.77 us
    pallas_call x1, Pallas kernels, pack_y(): pl.pallas_call(pack_y_kernel, out_shape=(shape, shape), in_specs=[pl.Bloc...  1.63 us
  transfers between devices with their start and end apart: 4, of which 2 were waited for; matrix products, arithmetic and copies ran while one was open for 0% of the time, Pallas kernels for 0%

commit v1 on v0

v1 whole, which is shorter than its diff:
```python
import functools

import jax
import jax.numpy as jnp
from jax import lax
from jax.experimental import pallas as pl
from jax.experimental.pallas import tpu as pltpu
from jax.sharding import PartitionSpec as P

VELOCITIES = (
    (0, 0, 0),
    (1, 0, 0),
    (-1, 0, 0),
    (0, 1, 0),
    (0, -1, 0),
    (0, 0, 1),
    (0, 0, -1),
    (1, 1, 0),
    (-1, -1, 0),
    (1, -1, 0),
    (-1, 1, 0),
    (1, 0, 1),
    (-1, 0, -1),
    (1, 0, -1),
    (-1, 0, 1),
    (0, 1, 1),
    (0, -1, -1),
    (0, 1, -1),
    (0, -1, 1),
)
OPPOSITE = (0, 2, 1, 4, 3, 6, 5, 8, 7, 10, 9, 12, 11, 14, 13, 16, 15, 18, 17)
K = 19
ROWS, COLS, NZ = 32, 32, 64
TILES = COLS * NZ // 128
EXT = 48
BASE = 8
SENS = 128
STARTS_WIDE = (7, 15, 23, 31, 33)
STARTS_OWN = (8, 16, 24, 32)
STARTS_INNER = (9, 17, 25, 31)
STARTS_EDGE = (7, 33)
X_SIDE = {"lo": (1, 7, 9, 11, 13), "hi": (2, 8, 10, 12, 14)}
Y_SIDE = {"lo": (3, 7, 10, 15, 17), "hi": (4, 8, 9, 16, 18)}
X_FIELDS = 32
Y_FIELDS = 7
F32 = jnp.float32
MB = 1024 * 1024
PREPARE_VMEM = 4 * MB
SMALL_VMEM = 4 * MB
HBM = pl.BlockSpec(memory_space=pltpu.HBM)
VMEM = pl.BlockSpec(memory_space=pltpu.VMEM)


def add(a, b):
    if a is None:
        return b
    return a if b is None else a + b


def sub(a, b):
    if b is None:
        return a
    return -b if a is None else a - b


def lanes():
    return lax.broadcasted_iota(jnp.int32, (8, 128), 1)


class Geometry:
    def __init__(self):
        lane = lanes()
        level = lane % NZ
        self.low = lane < NZ
        self.level = level.astype(F32)
        up = jnp.where(level == NZ - 1, -1, level + 1).astype(F32)
        self.raised = {0: self.level, 1: up, -1: self.level - 1.0}


def half_turn(value):
    return pltpu.roll(value, NZ, 1)


def from_next(geo, here, after):
    return jnp.where(geo.low, after, here)


def from_previous(geo, here, before):
    return jnp.where(geo.low, here, before)


def pull(geo, read, tile, after, before, position, number):
    cx, cy, cz = VELOCITIES[number]
    row = position + cx
    if cy == 0:
        value = read(tile, number, row)
        return pltpu.roll(value, (128 - cz) % 128, 1) if cz else value
    if cy == 1:
        value = from_next(geo, read(tile, number, row), read(after, number, row))
    else:
        value = from_previous(geo, read(tile, number, row), read(before, number, row))
    return pltpu.roll(value, NZ - cz, 1)


def incoming(geo, read, tops, tile, after, before, position, numbers):
    out = [None] * K
    for number in numbers:
        cx, cy, cz = VELOCITIES[number]
        value = pull(geo, read, tile, after, before, position, number)
        if number:
            blocked = geo.raised[cz] < tops(cy, position + cx)
            value = jnp.where(blocked, read(tile, OPPOSITE[number], position), value)
        out[number] = value
    return out


def moments(f):
    plus = [None] * K
    minus = [None] * K
    for number in range(1, K, 2):
        plus[number] = add(f[number], f[number + 1])
        minus[number] = sub(f[number], f[number + 1])
    sxy, dxy = add(plus[7], plus[9]), sub(plus[7], plus[9])
    sxz, dxz = add(plus[11], plus[13]), sub(plus[11], plus[13])
    syz, dyz = add(plus[15], plus[17]), sub(plus[15], plus[17])
    twice = [None if plus[n] is None else plus[n] + plus[n] for n in (1, 3, 5)]
    mxx = add(twice[0], add(sxy, sxz))
    myy = add(twice[1], add(sxy, syz))
    mzz = add(twice[2], add(sxz, syz))
    total = add(add(add(twice[0], twice[1]), twice[2]), add(add(sxy, sxz), syz))
    if f[0] is not None:
        total = add(12.0 * f[0], total)

    def axis(main, first, second):
        doubled = None if minus[main] is None else minus[main] + minus[main]
        return add(doubled, add(first, second))

    jx = axis(1, add(minus[7], minus[9]), add(minus[11], minus[13]))
    jy = axis(3, sub(minus[7], minus[9]), add(minus[15], minus[17]))
    jz = axis(5, sub(minus[11], minus[13]), sub(minus[15], minus[17]))
    return total, (jx, jy, jz), (mxx, myy, mzz, dxy, dxz, dyz)


def mul(a, b):
    return None if a is None else a * b


def collide(f, u, force, numbers, fluid):
    total, (jx, jy, jz), (mxx, myy, mzz, dxy, dxz, dyz) = moments(f)
    ux, uy, uz = u
    qx = add(add(mul(mxx, ux), mul(dxy, uy)), mul(dxz, uz))
    qy = add(add(mul(dxy, ux), mul(myy, uy)), mul(dyz, uz))
    qz = add(add(mul(dxz, ux), mul(dyz, uy)), mul(mzz, uz))
    speed = ux * ux + uy * uy + uz * uz
    scalar = total * (0.05 + 0.075 * speed) - 0.225 * (ux * qx + uy * qy + uz * qz)
    scaled = 0.15 * total
    vector = []
    for axis, (j, q) in enumerate(((jx, qx), (jy, qy), (jz, qz))):
        vector.append(sub(0.15 * add(j, 3.0 * q), scaled * u[axis]))
    if force is not None:
        scalar = scalar - (ux * force[0] + uy * force[1] + uz * force[2])
        vector = [vector[axis] + force[axis] for axis in range(3)]
    out = {}
    along = {}
    for number in numbers:
        c = VELOCITIES[number]
        pair = number if number % 2 else number - 1
        if number == 0:
            value = scalar
        else:
            if pair not in along:
                first = VELOCITIES[pair]
                cv = None
                for axis in range(3):
                    if first[axis] == 1:
                        cv = add(cv, vector[axis])
                    elif first[axis] == -1:
                        cv = sub(cv, vector[axis])
                along[pair] = cv
            value = scalar + along[pair] if number == pair else scalar - along[pair]
        if f[number] is not None:
            value = value - 0.8 * f[number]
        out[number] = jnp.where(fluid, value, 0.0)
    return out


def split3(value):
    high = value.astype(jnp.bfloat16)
    rest = value - high.astype(F32)
    middle = rest.astype(jnp.bfloat16)
    low = (rest - middle.astype(F32)).astype(jnp.bfloat16)
    return high, middle, low


def by_parity(parity, even, odd):
    pl.when(parity == 0)(even)
    pl.when(parity == 1)(odd)


def pack_x_kernel(adjoint, velocity, density, heights_hbm, cells_hbm, misfit_hbm, out_a, out_b,
                  rows_buf, u_buf, rho_buf, heights, cells, misfit, sems):
    copies = [
        pltpu.make_async_copy(heights_hbm, heights, sems.at[2, 0]),
        pltpu.make_async_copy(cells_hbm, cells, sems.at[2, 1]),
        pltpu.make_async_copy(misfit_hbm, misfit, sems.at[2, 2]),
    ]
    for side, start in ((0, 0), (1, ROWS - 8)):
        for tile in range(TILES):
            at = pl.ds(tile * 128, 128)
            copies.append(
                pltpu.make_async_copy(adjoint.at[:, pl.ds(start, 8), at], rows_buf.at[side, tile], sems.at[side, tile])
            )
        copies.append(pltpu.make_async_copy(velocity.at[1, :, pl.ds(start, 8), :], u_buf.at[side], sems.at[side, TILES]))
        copies.append(pltpu.make_async_copy(density.at[1, pl.ds(start, 8), :], rho_buf.at[side], sems.at[side, TILES + 1]))
    for copy in copies:
        copy.start()
    for copy in copies:
        copy.wait()
    flat = rows_buf.reshape(2, TILES, K * 8, 128)

    def pack(side, out):
        slot = 0 if side == "lo" else 1
        first = 0 if side == "lo" else 7
        second = 1 if side == "lo" else 6
        for tile in range(TILES):
            at = pl.ds(tile * 128, 128)
            out[0:8, at] = flat[slot, tile, pl.ds(first, 8, stride=8), :]
            out[8:16, at] = flat[slot, tile, pl.ds(64 + first, 8, stride=8), :]
            out[16:19, at] = flat[slot, tile, pl.ds(128 + first, 3, stride=8), :]
            for index, number in enumerate(X_SIDE[side]):
                out[19 + index : 20 + index, at] = rows_buf[slot, tile, number, second : second + 1, :]
        for axis in range(3):
            out[24 + axis : 25 + axis, :] = u_buf[slot, axis, first : first + 1, :]
        out[27:28, :] = rho_buf[slot, first : first + 1, :]
        edge = 0 if side == "lo" else ROWS - 1
        inner = 1 if side == "lo" else ROWS - 2
        out[28:29, 0:COLS] = heights[edge : edge + 1, :].astype(F32)
        out[28:29, 128 : 128 + COLS] = heights[inner : inner + 1, :].astype(F32)
        out[28:29, 256:384] = cells[0].astype(F32)
        for axis in range(3):
            out[28:29, 384 + 128 * axis : 512 + 128 * axis] = misfit[1, axis, 0]

    def even():
        pack("hi", out_a)
        pack("lo", out_b)

    def odd():
        pack("lo", out_a)
        pack("hi", out_b)

    by_parity(lax.axis_index("gx") % 2, even, odd)


def pack_x(adjoint, velocity, density, heights, cells, misfit):
    shape = jax.ShapeDtypeStruct((X_FIELDS, TILES * 128), F32)
    return pl.pallas_call(
        pack_x_kernel,
        out_shape=(shape, shape),
        in_specs=[HBM] * 6,
        out_specs=(VMEM, VMEM),
        scratch_shapes=[
            pltpu.VMEM((2, TILES, K, 8, 128), F32),
            pltpu.VMEM((2, 3, 8, TILES * 128), F32),
            pltpu.VMEM((2, 8, TILES * 128), F32),
            pltpu.VMEM((ROWS, COLS), jnp.int32),
            pltpu.VMEM((1, 1, SENS), jnp.int32),
            pltpu.VMEM((2, 3, 1, 1, SENS), F32),
            pltpu.SemaphoreType.DMA((3, TILES + 2)),
        ],
        compiler_params=pltpu.CompilerParams(vmem_limit_bytes=8 * MB),
        name="pack_x",
    )(adjoint, velocity, density, heights, cells, misfit)


def place_x(message, side, slot, tile, field, u):
    outer, inner = (BASE + ROWS, BASE + ROWS + 1) if side == "lo" else (BASE - 1, BASE - 2)
    flat = field.reshape(field.shape[0], K * EXT, 128)
    at = pl.ds(tile * 128, 128)
    flat[slot, pl.ds(outer, 8, stride=EXT), :] = message[0:8, at]
    flat[slot, pl.ds(8 * EXT + outer, 8, stride=EXT), :] = message[8:16, at]
    flat[slot, pl.ds(16 * EXT + outer, 3, stride=EXT), :] = message[16:19, at]
    for index, number in enumerate(X_SIDE[side]):
        field[slot, number, inner : inner + 1, :] = message[19 + index : 20 + index, at]
    for axis in range(3):
        u[slot, 1, axis, outer : outer + 1, :] = message[24 + axis : 25 + axis, at]


def place_tall(message, side, tall):
    outer, inner = (BASE + ROWS, BASE + ROWS + 1) if side == "lo" else (BASE - 1, BASE - 2)
    tall[outer : outer + 1, 0:COLS] = message[28:29, 0:COLS]
    tall[inner : inner + 1, 0:COLS] = message[28:29, 128 : 128 + COLS]


def edge_sensors(message, side):
    numbers = message[28:29, 256:384].astype(jnp.int32)
    here = numbers // (COLS * NZ) == (0 if side == "lo" else ROWS - 1)
    rows = [
        jnp.where(here, message[28:29, 384 + 128 * axis : 512 + 128 * axis], 0.0) for axis in range(3)
    ]
    parts = split3(jnp.concatenate(rows + [jnp.zeros((5, SENS), F32)], axis=0))
    return jnp.concatenate(parts + (jnp.zeros((8, SENS), jnp.bfloat16),), axis=0), numbers % (COLS * NZ)


def one_hot(lane, tile, width):
    cells = lax.broadcasted_iota(jnp.int32, (width, SENS), 0) + tile * 128
    return jnp.where(cells == lane, 1.0, 0.0).astype(jnp.bfloat16)


def product(left, right):
    return lax.dot_general(left, right, (((1,), (1,)), ((), ())), preferred_element_type=F32)


def place_force(message, side, sensors, slot, tile, force):
    outer = BASE + ROWS if side == "lo" else BASE - 1
    left, lane = sensors
    parts = product(left, one_hot(lane, tile, 128))
    total = parts[0:8] + (parts[8:16] + parts[16:24])
    scaled = total * (1.0 / message[27:28, pl.ds(tile * 128, 128)])
    for axis in range(3):
        force[slot, 1, axis, outer : outer + 1, :] = scaled[axis : axis + 1]


def column_tops(tall, tile, rows):
    at = slice(rows, rows + 8)
    low = lanes() < NZ
    left = jnp.broadcast_to(tall[at, 2 * tile : 2 * tile + 1], (8, 128))
    right = jnp.broadcast_to(tall[at, 2 * tile + 1 : 2 * tile + 2], (8, 128))
    return jnp.where(low, left, right)


def shifted_tops(geo, tops, tile, rows):
    at = pl.ds(rows, 8)
    after, before = (tile + 1) % (TILES + 1), (tile - 1) % (TILES + 1)
    here = tops[0, tile, at, :]
    tops[1, tile, at, :] = half_turn(from_next(geo, here, tops[0, after, at, :]))
    tops[2, tile, at, :] = half_turn(from_previous(geo, here, tops[0, before, at, :]))


def step(geo, number_of_step, source, target, u, force, tops, starts, tile, after, before):
    def read(where, number, row):
        return source[where, number, pl.ds(row, 8), :]

    def top(cy, row):
        return tops[cy % 3, tile, pl.ds(row, 8), :]

    for start in starts:
        at = pl.ds(start, 8)
        f = incoming(geo, read, top, tile, after, before, start, range(K))
        velocity = [u[tile, number_of_step, axis, at, :] for axis in range(3)]
        push = [force[tile, number_of_step, axis, at, :] for axis in range(3)]
        fluid = geo.level >= tops[0, tile, at, :]
        result = collide(f, velocity, push, range(K), fluid)
        for number in range(K):
            target[tile, number, at, :] = result[number]


WIDE = TILES + 1
FIELD = jax.ShapeDtypeStruct((WIDE, K, EXT, 128), F32)
VECTORS = jax.ShapeDtypeStruct((TILES, 2, 3, EXT, 128), F32)
TOPS = jax.ShapeDtypeStruct((3, WIDE, EXT, 128), F32)
TALL = jax.ShapeDtypeStruct((EXT, 128), F32)


def prepare_kernel(adjoint, velocity, density, heights_hbm, cells_hbm, misfit_hbm,
                   field, middle, u, force, tops, tall, rho, heights, cells, misfit, sems):
    own = pl.ds(BASE, ROWS)
    small = [
        pltpu.make_async_copy(heights_hbm, heights, sems.at[2, 1]),
        pltpu.make_async_copy(cells_hbm, cells, sems.at[2, 2]),
        pltpu.make_async_copy(misfit_hbm, misfit, sems.at[2, 3]),
    ]
    for copy in small:
        copy.start()
    loads = [pltpu.make_async_copy(density, rho, sems.at[2, 0])]
    for tile in range(TILES):
        at = pl.ds(tile * 128, 128)
        loads.append(pltpu.make_async_copy(adjoint.at[:, :, at], field.at[tile, :, own, :], sems.at[0, tile]))
    for tile in range(TILES):
        at = pl.ds(tile * 128, 128)
        loads.append(pltpu.make_async_copy(velocity.at[:, :, :, at], u.at[tile, :, :, own, :], sems.at[1, tile]))
    for copy in loads:
        copy.start()
    geo = Geometry()
    for copy in small:
        copy.wait()
    tall[BASE : BASE + ROWS, 0:COLS] = heights[...].astype(F32)
    for tile in range(TILES):
        for row in range(BASE, BASE + ROWS, 8):
            tops[0, tile, row : row + 8] = column_tops(tall, tile, row)
    for tile in range(1, TILES - 1):
        for row in range(BASE, BASE + ROWS, 8):
            shifted_tops(geo, tops, tile, row)

    numbers = cells[0]
    row = numbers // (COLS * NZ)
    lane = numbers % (COLS * NZ)
    here = lax.broadcasted_iota(jnp.int32, (ROWS, SENS), 0) == row
    parts = []
    for back in range(2):
        for axis in range(3):
            parts.append(split3(jnp.where(here, misfit[back, axis, 0], 0.0)))
    left = jnp.concatenate(
        [jnp.concatenate([part[index] for part in parts], axis=0) for index in range(3)], axis=1
    )
    loads[0].wait()
    for pair in range(TILES // 2):
        right = one_hot(lane, 2 * pair, 256)
        summed = product(left, jnp.concatenate([right, right, right], axis=1))
        for half in range(2):
            tile = 2 * pair + half
            at = pl.ds(tile * 128, 128)
            for back in range(2):
                inverse = 1.0 / rho[back, :, at]
                for axis in range(3):
                    first = (3 * back + axis) * ROWS
                    force[tile, back, axis, own, :] = (
                        summed[first : first + ROWS, 128 * half : 128 * half + 128] * inverse
                    )
    for copy in loads[1:]:
        copy.wait()

    def inner(tile, carry):
        step(geo, 1, field, middle, u, force, tops, STARTS_INNER, tile, tile + 1, tile - 1)
        return carry

    lax.fori_loop(1, TILES - 1, inner, 0)


def prepare(adjoint, velocity, density, heights, cells, misfit):
    return pl.pallas_call(
        prepare_kernel,
        out_shape=(FIELD, FIELD, VECTORS, VECTORS, TOPS, TALL),
        in_specs=[HBM] * 6,
        out_specs=(VMEM,) * 6,
        scratch_shapes=[
            pltpu.VMEM((2, ROWS, TILES * 128), F32),
            pltpu.VMEM((ROWS, COLS), jnp.int32),
            pltpu.VMEM((1, 1, SENS), jnp.int32),
            pltpu.VMEM((2, 3, 1, 1, SENS), F32),
            pltpu.SemaphoreType.DMA((3, TILES)),
        ],
        compiler_params=pltpu.CompilerParams(vmem_limit_bytes=PREPARE_VMEM),
        cost_estimate=pl.CostEstimate(flops=40_000_000, bytes_accessed=8_000_000, transcendentals=0),
        name="prepare",
    )(adjoint, velocity, density, heights, cells, misfit)


def pack_y_kernel(own_tall, all_field, all_u, all_force, msg_a, msg_b,
                  out_a, out_b, field, u, force, tall, tops, partial):
    slots = ((0, 0), (1, TILES - 1))
    own = pl.ds(BASE, ROWS)
    for slot, tile in slots:
        field[slot, :, own, :] = all_field[tile, :, own, :]
        u[slot, 1, :, own, :] = all_u[tile, 1, :, own, :]
        force[slot, 1, :, own, :] = all_force[tile, 1, :, own, :]
    tall[BASE : BASE + ROWS] = own_tall[BASE : BASE + ROWS]
    geo = Geometry()

    def from_x(low_msg, high_msg):
        for message, side in ((low_msg, "lo"), (high_msg, "hi")):
            place_tall(message, side, tall)
            sensors = edge_sensors(message, side)
            for slot, tile in slots:
                place_x(message, side, slot, tile, field, u)
                place_force(message, side, sensors, slot, tile, force)

    by_parity(lax.axis_index("gx") % 2, lambda: from_x(msg_a, msg_b), lambda: from_x(msg_b, msg_a))
    for slot, tile in slots:
        for row in range(0, EXT, 8):
            value = column_tops(tall, tile, row)
            tops[slot, 0, row : row + 8] = value
            tops[slot, 1, row : row + 8] = half_turn(value)

    def read(tile, number, row):
        return field[tile, number, pl.ds(row, 8), :]

    for slot, side in ((0, "lo"), (1, "hi")):
        inward = 1 if side == "lo" else -1
        numbers = [n for n in range(K) if VELOCITIES[n][1] in (0, inward)]
        for start in STARTS_WIDE:
            at = pl.ds(start, 8)

            def top(cy, row, slot=slot):
                return tops[slot, 0 if cy == 0 else 1, pl.ds(row, 8), :]

            f = incoming(geo, read, top, slot, slot, slot, start, numbers)
            velocity_here = [u[slot, 1, axis, at, :] for axis in range(3)]
            push = [force[slot, 1, axis, at, :] for axis in range(3)]
            fluid = geo.level >= tops[slot, 0, at, :]
            result = collide(f, velocity_here, push, Y_SIDE[side], fluid)
            for index, number in enumerate(Y_SIDE[side]):
                partial[slot, index, at, :] = result[number]

    def write(side, out):
        slot = 0 if side == "lo" else 1
        for start in range(0, 40, 8):
            at = pl.ds(start + BASE - 2, 8)
            pairs = [
                (field[slot, number, at, :], partial[slot, index, at, :])
                for index, number in enumerate(Y_SIDE[side])
            ]
            pairs.append((u[slot, 1, 0, at, :], u[slot, 1, 1, at, :]))
            pairs.append((u[slot, 1, 2, at, :], tops[slot, 0, at, :]))
            for index, (first, second) in enumerate(pairs):
                turned = half_turn(second)
                if side == "lo":
                    value = jnp.where(geo.low, first, turned)
                else:
                    value = jnp.where(geo.low, turned, first)
                out[index, start : start + 8, :] = value

    def even():
        write("hi", out_a)
        write("lo", out_b)

    def odd():
        write("lo", out_a)
        write("hi", out_b)

    by_parity(lax.axis_index("gy") % 2, even, odd)


def pack_y(heights, field, u, force, msg_a, msg_b):
    shape = jax.ShapeDtypeStruct((Y_FIELDS, 40, 128), F32)
    return pl.pallas_call(
        pack_y_kernel,
        out_shape=(shape, shape),
        in_specs=[VMEM] * 6,
        out_specs=(VMEM, VMEM),
        scratch_shapes=[
            pltpu.VMEM((2, K, EXT, 128), F32),
            pltpu.VMEM((2, 2, 3, EXT, 128), F32),
            pltpu.VMEM((2, 2, 3, EXT, 128), F32),
            pltpu.VMEM((EXT, 128), F32),
            pltpu.VMEM((2, 2, EXT, 128), F32),
            pltpu.VMEM((2, 5, EXT, 128), F32),
        ],
        compiler_params=pltpu.CompilerParams(vmem_limit_bytes=SMALL_VMEM),
        name="pack_y",
    )(heights, field, u, force, msg_a, msg_b)


def send_out(field, out, sems, tile):
    at = pl.ds(pl.multiple_of(tile * 128, 128), 128)
    return pltpu.make_async_copy(field.at[tile, :, pl.ds(BASE, ROWS), :], out.at[:, :, at], sems.at[tile])


def inner_kernel(own_tall, msg_a, msg_b, order, field_in, middle_in, u_in, force_in, tops_in,
                 field, middle, u, force, tops, out, tall, sems):
    del order, field_in, middle_in, u_in, force_in, tops_in
    geo = Geometry()
    tall[BASE : BASE + ROWS] = own_tall[BASE : BASE + ROWS]

    def from_x(low_msg, high_msg):
        for message, side in ((low_msg, "lo"), (high_msg, "hi")):
            place_tall(message, side, tall)
            sensors = edge_sensors(message, side)
            for tile in range(TILES):
                place_x(message, side, tile, tile, field, u)
                place_force(message, side, sensors, tile, tile, force)

    by_parity(lax.axis_index("gx") % 2, lambda: from_x(msg_a, msg_b), lambda: from_x(msg_b, msg_a))
    for tile in range(TILES):
        for row in (0, BASE + ROWS):
            tops[0, tile, row : row + 8] = column_tops(tall, tile, row)
    for tile in range(1, TILES - 1):
        for row in (0, BASE + ROWS):
            shifted_tops(geo, tops, tile, row)

    def edges(tile, carry):
        step(geo, 1, field, middle, u, force, tops, STARTS_EDGE, tile, tile + 1, tile - 1)
        return carry

    lax.fori_loop(1, TILES - 1, edges, 0)

    def second(tile, carry):
        step(geo, 0, middle, field, u, force, tops, STARTS_OWN, tile, tile + 1, tile - 1)
        send_out(field, out, sems, tile).start()
        return carry

    def sent(tile, carry):
        send_out(field, out, sems, tile).wait()
        return carry

    lax.fori_loop(2, TILES - 2, second, 0)
    lax.fori_loop(2, TILES - 2, sent, 0)


def inner_columns(heights, msg_a, msg_b, order, field, middle, u, force, tops, shape):
    return pl.pallas_call(
        inner_kernel,
        out_shape=(FIELD, FIELD, VECTORS, VECTORS, TOPS, jax.ShapeDtypeStruct(shape, F32)),
        in_specs=[VMEM] * 3 + [HBM] + [VMEM] * 5,
        out_specs=(VMEM,) * 5 + (HBM,),
        input_output_aliases={4: 0, 5: 1, 6: 2, 7: 3, 8: 4},
        scratch_shapes=[pltpu.VMEM((EXT, 128), F32), pltpu.SemaphoreType.DMA((TILES,))],
        compiler_params=pltpu.CompilerParams(vmem_limit_bytes=SMALL_VMEM),
        cost_estimate=pl.CostEstimate(flops=40_000_000, bytes_accessed=8_000_000, transcendentals=0),
        name="inner_columns",
    )(heights, msg_a, msg_b, order, field, middle, u, force, tops)


def outer_kernel(msg_a, msg_b, field_in, middle_in, u, force, tops_in, out_in,
                 field, middle, tops, out, side_partial, side_u, sems):
    del field_in, middle_in, tops_in, out_in
    geo = Geometry()

    def from_y(low_msg, high_msg):
        for start in range(0, 40, 8):
            at = pl.ds(start + BASE - 2, 8)
            for index in range(Y_FIELDS):
                low_value = low_msg[index, start : start + 8, :]
                high_value = high_msg[index, start : start + 8, :]
                low_turned, high_turned = half_turn(low_value), half_turn(high_value)
                if index < 5:
                    field[TILES, Y_SIDE["lo"][index], at, :] = low_value
                    field[TILES, Y_SIDE["hi"][index], at, :] = high_value
                    side_partial[0, index, at, :] = low_turned
                    side_partial[1, index, at, :] = high_turned
                else:
                    first = jnp.where(geo.low, low_value, high_value)
                    second = jnp.where(geo.low, low_turned, high_turned)
                    if index == 5:
                        side_u[0, at, :] = first
                        side_u[1, at, :] = second
                    else:
                        side_u[2, at, :] = first
                        tops[0, TILES, at, :] = second

    by_parity(lax.axis_index("gy") % 2, lambda: from_y(msg_a, msg_b), lambda: from_y(msg_b, msg_a))
    for tile in (0, TILES - 1, TILES):
        for row in range(0, EXT, 8):
            shifted_tops(geo, tops, tile, row)
    for tile, after, before in ((0, 1, TILES), (TILES - 1, TILES, TILES - 2)):
        step(geo, 1, field, middle, u, force, tops, STARTS_WIDE, tile, after, before)

    def read(where, number, row):
        return field[where, number, pl.ds(row, 8), :]

    def top(cy, row):
        return tops[cy % 3, TILES, pl.ds(row, 8), :]

    for slot, side, other in ((0, "lo", "hi"), (1, "hi", "lo")):
        for start in STARTS_WIDE:
            at = pl.ds(start, 8)
            f = incoming(geo, read, top, TILES, 0, TILES - 1, start, Y_SIDE[other])
            velocity = [side_u[axis, at, :] for axis in range(3)]
            fluid = geo.level >= tops[0, TILES, at, :]
            result = collide(f, velocity, None, Y_SIDE[side], fluid)
            for index, number in enumerate(Y_SIDE[side]):
                middle[TILES, number, at, :] = result[number] + side_partial[slot, index, at, :]

    last = (1, TILES - 2, 0, TILES - 1)
    for tile in last:
        before = TILES if tile == 0 else tile - 1
        step(geo, 0, middle, field, u, force, tops, STARTS_OWN, tile, tile + 1, before)
        send_out(field, out, sems, tile).start()
    for tile in last:
        send_out(field, out, sems, tile).wait()


def outer_columns(msg_a, msg_b, field, middle, u, force, tops, out):
    return pl.pallas_call(
        outer_kernel,
        out_shape=(FIELD, FIELD, TOPS, jax.ShapeDtypeStruct(out.shape, F32)),
        in_specs=[VMEM] * 7 + [HBM],
        out_specs=(VMEM,) * 3 + (HBM,),
        input_output_aliases={2: 0, 3: 1, 6: 2, 7: 3},
        scratch_shapes=[
            pltpu.VMEM((2, 5, EXT, 128), F32),
            pltpu.VMEM((3, EXT, 128), F32),
            pltpu.SemaphoreType.DMA((TILES,)),
        ],
        compiler_params=pltpu.CompilerParams(vmem_limit_bytes=SMALL_VMEM),
        name="outer_columns",
    )(msg_a, msg_b, field, middle, u, force, tops, out)


def partners(count, odd):
    if not odd:
        return [(i, i ^ 1) for i in range(count)]
    return [(i, (i - 1) % count if i % 2 == 0 else (i + 1) % count) for i in range(count)]


def swap(value, axis, odd):
    return lax.ppermute(value, axis, partners(lax.axis_size(axis), odd))


def per_device(adjoint, velocity, density, heights, cells, misfit):
    args = [
        pltpu.with_memory_space_constraint(value, pltpu.HBM)
        for value in (adjoint, velocity, density, heights, cells, misfit)
    ]
    x_a, x_b = pack_x(*args)
    x_a, x_b = swap(x_a, "gx", False), swap(x_b, "gx", True)
    field, middle, u, force, tops, tall = prepare(*args)
    own_a, own_b = pack_y(tall, field, u, force, x_a, x_b)
    y_a, y_b = swap(own_a, "gy", False), swap(own_b, "gy", True)
    field, middle, u, force, tops, out = inner_columns(
        tall, x_a, x_b, own_a, field, middle, u, force, tops, adjoint.shape
    )
    return outer_columns(y_a, y_b, field, middle, u, force, tops, out)[3]


def solution(mesh):
    return jax.shard_map(
        per_device,
        mesh=mesh,
        in_specs=(
            P(None, "gx", "gy"),
            P(None, None, "gx", "gy"),
            P(None, "gx", "gy"),
            P("gx", "gy"),
            P("gx", "gy", None),
            P(None, None, "gx", "gy", None),
        ),
        out_specs=P(None, "gx", "gy"),
        check_vma=False,
    )
```

time: 48 us -> 29.3 us (0.61)
  waiting for transfers between devices: 7.13 us -> 0.01 us
  local copies, waits for them, and re-layouts: 6.95 us -> 0 us
  Pallas kernels: 22.9 us -> 18.6 us
    ppermute x4, waiting for transfers between devices: 7.13 us -> 0.01 us  [swap(): return lax.ppermute(value, axis, partners(lax.axis_size(axis), odd))]
    unnamed x22 -> x0, local copies, waits for them, and re-layouts: 6.95 us -> none
    pallas_call x3 -> x5, Pallas kernels: 22.9 us -> 18.6 us  [the longest x1 6.58 us: prepare(): pl.pallas_call(prepare_kernel, out_shape=(FIELD, FIELD, VECTORS, VECTORS,...]
  transfers between devices with their start and end apart: 4 -> 4, of which waited for: 2 -> 0; matrix products, arithmetic and copies ran while one was open for 0% -> 0% of each run, Pallas kernels for 0% -> 44%
where the time goes in v1:
time: 29.3 us; the launch traced here: 29.1 us
  Pallas kernels  18.6 us (63%)
  starting transfers between devices  10.4 us (35%)
    ppermute x4, starting transfers between devices, swap(): return lax.ppermute(value, axis, partners(lax.axis_size(axis), odd))  10.4 us
    pallas_call x1, Pallas kernels, prepare(): pl.pallas_call(prepare_kernel, out_shape=(FIELD, FIELD, VECTORS, VECTORS,...  6.58 us
    pallas_call x1, Pallas kernels, inner_columns(): pl.pallas_call(inner_kernel, out_shape=(FIELD, FIELD, VECTORS, VECTORS, T...  6.32 us
    pallas_call x1, Pallas kernels, pack_x(): pl.pallas_call(pack_x_kernel, out_shape=(shape, shape), in_specs=[HBM] *...  2.57 us
    pallas_call x1, Pallas kernels, outer_columns(): pl.pallas_call(outer_kernel, out_shape=(FIELD, FIELD, TOPS, jax.ShapeDtyp...  2.35 us
    pallas_call x1, Pallas kernels, pack_y(): pl.pallas_call(pack_y_kernel, out_shape=(shape, shape), in_specs=[VMEM] *...  0.75 us
  transfers between devices with their start and end apart: 4, of which 0 were waited for; matrix products, arithmetic and copies ran while one was open for 0% of the time, Pallas kernels for 44%

profile of v1, /device:TPU:0, one launch (start us, length us, event | category | flops | bytes accessed | tf_op | source)
XLA Modules:
  0.0 29.1 jit_solution(14814325090122043750)
XLA Ops:
  0.0 2.6 %pack_x.1 = (f32[32,2048]{1,0:T(8,128)S(1)}, f32[32,2048]{1,0:T(8,128)S(1)}) custom-call(f32[19,32,2048]{2,1,0:T(8,128)} %adjoint.3, f32[2,3,32,2048]{3,2,1,0:T(8,128)} %velocity.3, f32[2,32,2048]{2,1,0:T(8,128)} %density.3, s32[32,32]{1,0:T(8,128)} %heights_hbm.3, s32[1,1,128]{2,1,0:T(1,128)} %cells_hbm.3, f32[2,3,1,1,128]{4,3,2,1,0:T(1,128)} %misfit_hbm.3), custom_call_target="tpu_custom_call" | custom-call | tf_op jit(solution)/shard_map/pack_x/pallas_call | solution.py:256
  2.6 0.1 collective-permute-start
  2.7 3.2 %collective-permute-start.1 = (f32[32,2048]{1,0:T(8,128)S(1)}, f32[32,2048]{1,0:T(8,128)S(1)}, u32[]{:S(2)}, u32[]{:S(2)}) collective-permute-start(f32[32,2048]{1,0:T(8,128)S(1)} %get-tuple-element.27), channel_id=1, source_target_pairs={{0,112},{16,32},{32,16},{48,64},{64,48},{80,96},{96,80},{112,0},{1... | collective-permute-start | bytes 786440 | tf_op jit(solution)/shard_map/ppermute | solution.py:686
  5.9 6.6 %prepare.1 = (f32[17,19,48,128]{3,2,1,0:T(8,128)S(1)}, f32[17,19,48,128]{3,2,1,0:T(8,128)S(1)}, f32[16,2,3,48,128]{4,3,2,1,0:T(8,128)S(1)}, f32[16,2,3,48,128]{4...) custom-call(f32[19,32,2048]{2,1,0:T(8,128)} %adjoint.3, f32[2,3,32,2048]{3,2,1,0:T(8,128)} %velocity.3, ...), custom_call_target="tpu_custom_call" | custom-call | flops 40000000 | bytes 8000000 | tf_op jit(solution)/shard_map/prepare/pallas_call | solution.py:430
  12.5 0.0 collective-permute-done.msg_a
  12.5 0.0 collective-permute-done.1.msg_b
  12.5 0.8 %pack_y.1 = (f32[7,40,128]{2,1,0:T(8,128)S(1)}, f32[7,40,128]{2,1,0:T(8,128)S(1)}) custom-call(f32[48,128]{1,0:T(8,128)S(1)} %get-tuple-element.22.own_tall, f32[17,19,48,128]{3,2,1,0:T(8,128)S(1)} %get-tuple-element.23.all_field.field_in, f32[16,2,3,48,128]{4,3,2,1,0:T(8,128)S(1)} %get-tuple-element.24.all_u.u_in, ...), custom_call_target="tpu_custom_call" | custom-call | tf_op jit(solution)/shard_map/pack_y/pallas_call | solution.py:525
  13.2 1.6 %collective-permute-start.2 = (f32[7,40,128]{2,1,0:T(8,128)S(1)}, f32[7,40,128]{2,1,0:T(8,128)S(1)}, u32[]{:S(2)}, u32[]{:S(2)}) collective-permute-start(f32[7,40,128]{2,1,0:T(8,128)S(1)} %get-tuple-element.28.order), channel_id=1, source_target_pairs={{0,1},{1,0},{2,3},{3,2},{4,5},{5,4},{6,7},{7,6},{8,9},{9,8},{10,11... | collective-permute-start | bytes 430088 | tf_op jit(solution)/shard_map/ppermute | solution.py:686
  14.8 5.6 %collective-permute-start.3 = (f32[7,40,128]{2,1,0:T(8,128)S(1)}, f32[7,40,128]{2,1,0:T(8,128)S(1)}, u32[]{:S(2)}, u32[]{:S(2)}) collective-permute-start(f32[7,40,128]{2,1,0:T(8,128)S(1)} %get-tuple-element.29), channel_id=1, source_target_pairs={{0,15},{1,2},{2,1},{3,4},{4,3},{5,6},{6,5},{7,8},{8,7},{9,10},{10,... | collective-permute-start | bytes 430088 | tf_op jit(solution)/shard_map/ppermute | solution.py:686
  20.4 6.3 %inner_columns.1 = (f32[17,19,48,128]{3,2,1,0:T(8,128)S(1)}, f32[17,19,48,128]{3,2,1,0:T(8,128)S(1)}, f32[16,2,3,48,128]{4,3,2,1,0:T(8,128)S(1)}, f32[16,2,3,48,...) custom-call(f32[48,128]{1,0:T(8,128)S(1)} %get-tuple-element.22.own_, ...), custom_call_target="tpu_custom_call", output_to_operand_aliasing={{0}: (4, {}), {1}: (5, {}), {2}: (6, {}), {3}: (7, {}), {4}... | custom-call | flops 40000000 | bytes 8000000 | tf_op jit(solution)/shard_map/inner_columns/pallas_call | solution.py:590
  26.7 0.0 collective-permute-done.2.msg_a
  26.7 0.0 collective-permute-done.3.msg_b
  26.7 2.3 %outer_columns.1 = (f32[17,19,48,128]{3,2,1,0:T(8,128)S(1)}, f32[17,19,48,128]{3,2,1,0:T(8,128)S(1)}, f32[3,17,48,128]{3,2,1,0:T(8,128)S(1)}, f32[19,32,2048]{2,1,0:T(8,128)}) custom-call(f32[7,40,128]{2,1,0:T(8,128)S(1)} %collective-permute-done.2.msg_a, ...), custom_call_target="tpu_custom_call", output_to_operand_aliasing={{0}: (2, {}), {1}: (3, {}), {2}: (6, {}), {3}: (7, {})} | custom-call | tf_op jit(solution)/shard_map/outer_columns/pallas_call | solution.py:663
Async XLA Ops:
  2.6 9.9 %collective-permute-start = (f32[32,2048]{1,0:T(8,128)S(1)}, f32[32,2048]{1,0:T(8,128)S(1)}, u32[]{:S(2)}, u32[]{:S(2)}) collective-permute-start(f32[32,2048]{1,0:T(8,128)S(1)} %get-tuple-element.26), channel_id=1, source_target_pairs={{0,16},{16,0},{32,48},{48,32},{64,80},{80,64},{96,112},{112,96},{1... | collective-permute-start | bytes 786440 | tf_op jit(solution)/shard_map/ppermute | solution.py:686
  2.7 9.8 %collective-permute-start.1 = (f32[32,2048]{1,0:T(8,128)S(1)}, f32[32,2048]{1,0:T(8,128)S(1)}, u32[]{:S(2)}, u32[]{:S(2)}) collective-permute-start(f32[32,2048]{1,0:T(8,128)S(1)} %get-tuple-element.27), channel_id=1, source_target_pairs={{0,112},{16,32},{32,16},{48,64},{64,48},{80,96},{96,80},{112,0},{1... | collective-permute-start | bytes 786440 | tf_op jit(solution)/shard_map/ppermute | solution.py:686
  13.2 13.5 %collective-permute-start.2 = (f32[7,40,128]{2,1,0:T(8,128)S(1)}, f32[7,40,128]{2,1,0:T(8,128)S(1)}, u32[]{:S(2)}, u32[]{:S(2)}) collective-permute-start(f32[7,40,128]{2,1,0:T(8,128)S(1)} %get-tuple-element.28.order), channel_id=1, source_target_pairs={{0,1},{1,0},{2,3},{3,2},{4,5},{5,4},{6,7},{7,6},{8,9},{9,8},{10,11... | collective-permute-start | bytes 430088 | tf_op jit(solution)/shard_map/ppermute | solution.py:686
  14.8 11.9 %collective-permute-start.3 = (f32[7,40,128]{2,1,0:T(8,128)S(1)}, f32[7,40,128]{2,1,0:T(8,128)S(1)}, u32[]{:S(2)}, u32[]{:S(2)}) collective-permute-start(f32[7,40,128]{2,1,0:T(8,128)S(1)} %get-tuple-element.29), channel_id=1, source_target_pairs={{0,15},{1,2},{2,1},{3,4},{4,3},{5,6},{6,5},{7,8},{8,7},{9,10},{10,... | collective-permute-start | bytes 430088 | tf_op jit(solution)/shard_map/ppermute | solution.py:686

commit v2 on v1

--- a/solution.py
+++ b/solution.py
@@ -145,25 +145,31 @@
     return None if a is None else a * b
 
 
-def collide(f, u, force, numbers, fluid):
+SCALES = {1: (1.0, -1.25), 0: (-0.8, 1.0)}
+
+
+def collide(f, u, force, numbers, number_of_step):
+    read_scale, write_scale = SCALES[number_of_step]
+    scale = read_scale * write_scale
     total, (jx, jy, jz), (mxx, myy, mzz, dxy, dxz, dyz) = moments(f)
     ux, uy, uz = u
-    qx = add(add(mul(mxx, ux), mul(dxy, uy)), mul(dxz, uz))
-    qy = add(add(mul(dxy, ux), mul(myy, uy)), mul(dyz, uz))
-    qz = add(add(mul(dxz, ux), mul(dyz, uy)), mul(mzz, uz))
+    sx, sy, sz = (0.225 * scale) * ux, (0.225 * scale) * uy, (0.225 * scale) * uz
+    qx = add(add(mul(mxx, sx), mul(dxy, sy)), mul(dxz, sz))
+    qy = add(add(mul(dxy, sx), mul(myy, sy)), mul(dyz, sz))
+    qz = add(add(mul(dxz, sx), mul(dyz, sy)), mul(mzz, sz))
+    q = (qx, qy, qz)
+    pushed = q if force is None else [q[axis] + force[axis] for axis in range(3)]
     speed = ux * ux + uy * uy + uz * uz
-    scalar = total * (0.05 + 0.075 * speed) - 0.225 * (ux * qx + uy * qy + uz * qz)
-    scaled = 0.15 * total
+    scalar = total * (0.05 * scale + (0.075 * scale) * speed)
+    scalar = scalar - (ux * pushed[0] + uy * pushed[1] + uz * pushed[2])
+    scaled = (0.15 * scale) * total
     vector = []
-    for axis, (j, q) in enumerate(((jx, qx), (jy, qy), (jz, qz))):
-        vector.append(sub(0.15 * add(j, 3.0 * q), scaled * u[axis]))
-    if force is not None:
-        scalar = scalar - (ux * force[0] + uy * force[1] + uz * force[2])
-        vector = [vector[axis] + force[axis] for axis in range(3)]
+    for axis, j in enumerate((jx, jy, jz)):
+        value = q[axis] + pushed[axis] - scaled * u[axis]
+        vector.append(add(mul(j, 0.15 * scale), value))
     out = {}
     along = {}
     for number in numbers:
-        c = VELOCITIES[number]
         pair = number if number % 2 else number - 1
         if number == 0:
             value = scalar
@@ -179,26 +185,32 @@
                 along[pair] = cv
             value = scalar + along[pair] if number == pair else scalar - along[pair]
         if f[number] is not None:
-            value = value - 0.8 * f[number]
-        out[number] = jnp.where(fluid, value, 0.0)
+            value = value + (f[number] if number_of_step == 1 else (-0.8 * scale) * f[number])
+        out[number] = value
     return out
 
 
-def split3(value):
+def split(value):
     high = value.astype(jnp.bfloat16)
-    rest = value - high.astype(F32)
-    middle = rest.astype(jnp.bfloat16)
-    low = (rest - middle.astype(F32)).astype(jnp.bfloat16)
-    return high, middle, low
-
-
-def by_parity(parity, even, odd):
-    pl.when(parity == 0)(even)
-    pl.when(parity == 1)(odd)
+    return high, (value - high.astype(F32)).astype(jnp.bfloat16)
+
+
+def one_hot(lane, tile, width):
+    cells = lax.broadcasted_iota(jnp.int32, (width, SENS), 0) + tile * 128
+    return jnp.where(cells == lane, 1.0, 0.0).astype(jnp.bfloat16)
+
+
+def product(left, right):
+    return lax.dot_general(left, right, (((1,), (1,)), ((), ())), preferred_element_type=F32)
+
+
+def by_parity(parity, upper, lower):
+    pl.when(parity == 1)(upper)
+    pl.when(parity == 0)(lower)
 
 
 def pack_x_kernel(adjoint, velocity, density, heights_hbm, cells_hbm, misfit_hbm, out_a, out_b,
-                  rows_buf, u_buf, rho_buf, heights, cells, misfit, sems):
+                  rows_buf, u_buf, rho_buf, heights, cells, misfit, edge_force, sems):
     copies = [
         pltpu.make_async_copy(heights_hbm, heights, sems.at[2, 0]),
         pltpu.make_async_copy(cells_hbm, cells, sems.at[2, 1]),
@@ -214,7 +226,22 @@
         copies.append(pltpu.make_async_copy(density.at[1, pl.ds(start, 8), :], rho_buf.at[side], sems.at[side, TILES + 1]))
     for copy in copies:
         copy.start()
-    for copy in copies:
+    for copy in copies[:3]:
+        copy.wait()
+    numbers = cells[0]
+    lane = numbers % (COLS * NZ)
+    parts = []
+    for edge in (0, ROWS - 1):
+        here = numbers // (COLS * NZ) == edge
+        rows = [jnp.where(here, SCALES[1][1] * misfit[1, axis, 0], 0.0) for axis in range(3)]
+        parts.append(split(jnp.concatenate(rows + [jnp.zeros((5, SENS), F32)], axis=0)))
+    left = jnp.concatenate(
+        [jnp.concatenate([part[index] for part in parts], axis=0) for index in range(2)], axis=1
+    )
+    for pair in range(TILES // 2):
+        right = one_hot(lane, 2 * pair, 256)
+        edge_force[:, pl.ds(256 * pair, 256)] = product(left, jnp.concatenate([right, right], axis=1))
+    for copy in copies[3:]:
         copy.wait()
     flat = rows_buf.reshape(2, TILES, K * 8, 128)
 
@@ -229,26 +256,24 @@
             out[16:19, at] = flat[slot, tile, pl.ds(128 + first, 3, stride=8), :]
             for index, number in enumerate(X_SIDE[side]):
                 out[19 + index : 20 + index, at] = rows_buf[slot, tile, number, second : second + 1, :]
+        inverse = 1.0 / rho_buf[slot, first : first + 1, :]
+        out[24:27, :] = edge_force[8 * slot : 8 * slot + 3, :] * inverse
         for axis in range(3):
-            out[24 + axis : 25 + axis, :] = u_buf[slot, axis, first : first + 1, :]
-        out[27:28, :] = rho_buf[slot, first : first + 1, :]
+            out[27 + axis : 28 + axis, :] = u_buf[slot, axis, first : first + 1, :]
         edge = 0 if side == "lo" else ROWS - 1
         inner = 1 if side == "lo" else ROWS - 2
-        out[28:29, 0:COLS] = heights[edge : edge + 1, :].astype(F32)
-        out[28:29, 128 : 128 + COLS] = heights[inner : inner + 1, :].astype(F32)
-        out[28:29, 256:384] = cells[0].astype(F32)
-        for axis in range(3):
-            out[28:29, 384 + 128 * axis : 512 + 128 * axis] = misfit[1, axis, 0]
-
-    def even():
+        out[30:31, 0:COLS] = heights[edge : edge + 1, :].astype(F32)
+        out[30:31, 128 : 128 + COLS] = heights[inner : inner + 1, :].astype(F32)
+
+    def upper():
         pack("hi", out_a)
         pack("lo", out_b)
 
-    def odd():
+    def lower():
         pack("lo", out_a)
         pack("hi", out_b)
 
-    by_parity(lax.axis_index("gx") % 2, even, odd)
+    by_parity(lax.axis_index("gx") % 2, upper, lower)
 
 
 def pack_x(adjoint, velocity, density, heights, cells, misfit):
@@ -265,6 +290,7 @@
             pltpu.VMEM((ROWS, COLS), jnp.int32),
             pltpu.VMEM((1, 1, SENS), jnp.int32),
             pltpu.VMEM((2, 3, 1, 1, SENS), F32),
+            pltpu.VMEM((16, TILES * 128), F32),
             pltpu.SemaphoreType.DMA((3, TILES + 2)),
         ],
         compiler_params=pltpu.CompilerParams(vmem_limit_bytes=8 * MB),
@@ -272,7 +298,7 @@
     )(adjoint, velocity, density, heights, cells, misfit)
 
 
-def place_x(message, side, slot, tile, field, u):
+def place_x(message, side, slot, tile, field, u, force):
     outer, inner = (BASE + ROWS, BASE + ROWS + 1) if side == "lo" else (BASE - 1, BASE - 2)
     flat = field.reshape(field.shape[0], K * EXT, 128)
     at = pl.ds(tile * 128, 128)
@@ -282,42 +308,14 @@
     for index, number in enumerate(X_SIDE[side]):
         field[slot, number, inner : inner + 1, :] = message[19 + index : 20 + index, at]
     for axis in range(3):
-        u[slot, 1, axis, outer : outer + 1, :] = message[24 + axis : 25 + axis, at]
+        force[slot, 1, axis, outer : outer + 1, :] = message[24 + axis : 25 + axis, at]
+        u[slot, 1, axis, outer : outer + 1, :] = message[27 + axis : 28 + axis, at]
 
 
 def place_tall(message, side, tall):
     outer, inner = (BASE + ROWS, BASE + ROWS + 1) if side == "lo" else (BASE - 1, BASE - 2)
-    tall[outer : outer + 1, 0:COLS] = message[28:29, 0:COLS]
-    tall[inner : inner + 1, 0:COLS] = message[28:29, 128 : 128 + COLS]
-
-
-def edge_sensors(message, side):
-    numbers = message[28:29, 256:384].astype(jnp.int32)
-    here = numbers // (COLS * NZ) == (0 if side == "lo" else ROWS - 1)
-    rows = [
-        jnp.where(here, message[28:29, 384 + 128 * axis : 512 + 128 * axis], 0.0) for axis in range(3)
-    ]
-    parts = split3(jnp.concatenate(rows + [jnp.zeros((5, SENS), F32)], axis=0))
-    return jnp.concatenate(parts + (jnp.zeros((8, SENS), jnp.bfloat16),), axis=0), numbers % (COLS * NZ)
-
-
-def one_hot(lane, tile, width):
-    cells = lax.broadcasted_iota(jnp.int32, (width, SENS), 0) + tile * 128
-    return jnp.where(cells == lane, 1.0, 0.0).astype(jnp.bfloat16)
-
-
-def product(left, right):
-    return lax.dot_general(left, right, (((1,), (1,)), ((), ())), preferred_element_type=F32)
-
-
-def place_force(message, side, sensors, slot, tile, force):
-    outer = BASE + ROWS if side == "lo" else BASE - 1
-    left, lane = sensors
-    parts = product(left, one_hot(lane, tile, 128))
-    total = parts[0:8] + (parts[8:16] + parts[16:24])
-    scaled = total * (1.0 / message[27:28, pl.ds(tile * 128, 128)])
-    for axis in range(3):
-        force[slot, 1, axis, outer : outer + 1, :] = scaled[axis : axis + 1]
+    tall[outer : outer + 1, 0:COLS] = message[30:31, 0:COLS]
+    tall[inner : inner + 1, 0:COLS] = message[30:31, 128 : 128 + COLS]
 
 
 def column_tops(tall, tile, rows):
@@ -348,10 +346,15 @@
         f = incoming(geo, read, top, tile, after, before, start, range(K))
         velocity = [u[tile, number_of_step, axis, at, :] for axis in range(3)]
         push = [force[tile, number_of_step, axis, at, :] for axis in range(3)]
-        fluid = geo.level >= tops[0, tile, at, :]
-        result = collide(f, velocity, push, range(K), fluid)
-        for number in range(K):
-            target[tile, number, at, :] = result[number]
+        result = collide(f, velocity, push, range(K), number_of_step)
+        if number_of_step:
+            for number in range(K):
+                target[tile, number, at, :] = result[number]
+        else:
+            fluid = geo.level >= tops[0, tile, at, :]
+            for number in range(K):
+                target[tile, number, at, :] = jnp.zeros((8, 128), F32)
+                pltpu.store(target.at[tile, number, at, :], result[number], mask=fluid)
 
 
 WIDE = TILES + 1
@@ -371,15 +374,23 @@
     ]
     for copy in small:
         copy.start()
-    loads = [pltpu.make_async_copy(density, rho, sems.at[2, 0])]
+    load_rho = pltpu.make_async_copy(density, rho, sems.at[2, 0])
+    load_rho.start()
+
+    def load(tile):
+        at = pl.ds(pl.multiple_of(tile * 128, 128), 128)
+        return (
+            pltpu.make_async_copy(adjoint.at[:, :, at], field.at[tile, :, own, :], sems.at[0, tile]),
+            pltpu.make_async_copy(velocity.at[:, :, :, at], u.at[tile, :, :, own, :], sems.at[1, tile]),
+        )
+
+    def arrived(tile):
+        for copy in load(tile):
+            copy.wait()
+
     for tile in range(TILES):
-        at = pl.ds(tile * 128, 128)
-        loads.append(pltpu.make_async_copy(adjoint.at[:, :, at], field.at[tile, :, own, :], sems.at[0, tile]))
-    for tile in range(TILES):
-        at = pl.ds(tile * 128, 128)
-        loads.append(pltpu.make_async_copy(velocity.at[:, :, :, at], u.at[tile, :, :, own, :], sems.at[1, tile]))
-    for copy in loads:
-        copy.start()
+        for copy in load(tile):
+            copy.start()
     geo = Geometry()
     for copy in small:
         copy.wait()
@@ -398,14 +409,14 @@
     parts = []
     for back in range(2):
         for axis in range(3):
-            parts.append(split3(jnp.where(here, misfit[back, axis, 0], 0.0)))
+            parts.append(split(jnp.where(here, SCALES[back][1] * misfit[back, axis, 0], 0.0)))
     left = jnp.concatenate(
-        [jnp.concatenate([part[index] for part in parts], axis=0) for index in range(3)], axis=1
+        [jnp.concatenate([part[index] for part in parts], axis=0) for index in range(2)], axis=1
     )
-    loads[0].wait()
+    load_rho.wait()
     for pair in range(TILES // 2):
         right = one_hot(lane, 2 * pair, 256)
-        summed = product(left, jnp.concatenate([right, right, right], axis=1))
+        summed = product(left, jnp.concatenate([right, right], axis=1))
         for half in range(2):
             tile = 2 * pair + half
             at = pl.ds(tile * 128, 128)
@@ -416,10 +427,11 @@
                     force[tile, back, axis, own, :] = (
                         summed[first : first + ROWS, 128 * half : 128 * half + 128] * inverse
                     )
-    for copy in loads[1:]:
-        copy.wait()
+    arrived(0)
+    arrived(1)
 
     def inner(tile, carry):
+        arrived(tile + 1)
         step(geo, 1, field, middle, u, force, tops, STARTS_INNER, tile, tile + 1, tile - 1)
         return carry
 
@@ -459,10 +471,8 @@
     def from_x(low_msg, high_msg):
         for message, side in ((low_msg, "lo"), (high_msg, "hi")):
             place_tall(message, side, tall)
-            sensors = edge_sensors(message, side)
             for slot, tile in slots:
-                place_x(message, side, slot, tile, field, u)
-                place_force(message, side, sensors, slot, tile, force)
+                place_x(message, side, slot, tile, field, u, force)
 
     by_parity(lax.axis_index("gx") % 2, lambda: from_x(msg_a, msg_b), lambda: from_x(msg_b, msg_a))
     for slot, tile in slots:
@@ -486,8 +496,7 @@
             f = incoming(geo, read, top, slot, slot, slot, start, numbers)
             velocity_here = [u[slot, 1, axis, at, :] for axis in range(3)]
             push = [force[slot, 1, axis, at, :] for axis in range(3)]
-            fluid = geo.level >= tops[slot, 0, at, :]
-            result = collide(f, velocity_here, push, Y_SIDE[side], fluid)
+            result = collide(f, velocity_here, push, Y_SIDE[side], 1)
             for index, number in enumerate(Y_SIDE[side]):
                 partial[slot, index, at, :] = result[number]
 
@@ -509,15 +518,15 @@
                     value = jnp.where(geo.low, turned, first)
                 out[index, start : start + 8, :] = value
 
-    def even():
+    def upper():
         write("hi", out_a)
         write("lo", out_b)
 
-    def odd():
+    def lower():
         write("lo", out_a)
         write("hi", out_b)
 
-    by_parity(lax.axis_index("gy") % 2, even, odd)
+    by_parity(lax.axis_index("gy") % 2, upper, lower)
 
 
 def pack_y(heights, field, u, force, msg_a, msg_b):
@@ -554,10 +563,8 @@
     def from_x(low_msg, high_msg):
         for message, side in ((low_msg, "lo"), (high_msg, "hi")):
             place_tall(message, side, tall)
-            sensors = edge_sensors(message, side)
             for tile in range(TILES):
-                place_x(message, side, tile, tile, field, u)
-                place_force(message, side, sensors, tile, tile, force)
+                place_x(message, side, tile, tile, field, u, force)
 
     by_parity(lax.axis_index("gx") % 2, lambda: from_x(msg_a, msg_b), lambda: from_x(msg_b, msg_a))
     for tile in range(TILES):
@@ -567,13 +574,14 @@
         for row in (0, BASE + ROWS):
             shifted_tops(geo, tops, tile, row)
 
-    def edges(tile, carry):
+    def edges(tile):
         step(geo, 1, field, middle, u, force, tops, STARTS_EDGE, tile, tile + 1, tile - 1)
-        return carry
-
-    lax.fori_loop(1, TILES - 1, edges, 0)
+
+    edges(1)
+    edges(2)
 
     def second(tile, carry):
+        edges(tile + 1)
         step(geo, 0, middle, field, u, force, tops, STARTS_OWN, tile, tile + 1, tile - 1)
         send_out(field, out, sems, tile).start()
         return carry
@@ -645,8 +653,7 @@
             at = pl.ds(start, 8)
             f = incoming(geo, read, top, TILES, 0, TILES - 1, start, Y_SIDE[other])
             velocity = [side_u[axis, at, :] for axis in range(3)]
-            fluid = geo.level >= tops[0, TILES, at, :]
-            result = collide(f, velocity, None, Y_SIDE[side], fluid)
+            result = collide(f, velocity, None, Y_SIDE[side], 1)
             for index, number in enumerate(Y_SIDE[side]):
                 middle[TILES, number, at, :] = result[number] + side_partial[slot, index, at, :]
 
@@ -692,10 +699,10 @@
         for value in (adjoint, velocity, density, heights, cells, misfit)
     ]
     x_a, x_b = pack_x(*args)
-    x_a, x_b = swap(x_a, "gx", False), swap(x_b, "gx", True)
+    x_a, x_b = swap(x_a, "gx", True), swap(x_b, "gx", False)
     field, middle, u, force, tops, tall = prepare(*args)
     own_a, own_b = pack_y(tall, field, u, force, x_a, x_b)
-    y_a, y_b = swap(own_a, "gy", False), swap(own_b, "gy", True)
+    y_a, y_b = swap(own_a, "gy", True), swap(own_b, "gy", False)
     field, middle, u, force, tops, out = inner_columns(
         tall, x_a, x_b, own_a, field, middle, u, force, tops, adjoint.shape
     )

time: 29.3 us -> 25.8 us (0.88)
  the two profiles are of different devices: /device:TPU:0 before, /device:TPU:1 now
where the time goes in v2:
time: 25.8 us; the launch traced here: 25.5 us
  Pallas kernels  15.4 us (60%)
  starting transfers between devices  10.1 us (39%)
    ppermute x4, starting transfers between devices, swap(): return lax.ppermute(value, axis, partners(lax.axis_size(axis), odd))  10.1 us
    pallas_call x1, Pallas kernels, inner_columns(): pl.pallas_call(inner_kernel, out_shape=(FIELD, FIELD, VECTORS, VECTORS, T...  5.17 us
    pallas_call x1, Pallas kernels, prepare(): pl.pallas_call(prepare_kernel, out_shape=(FIELD, FIELD, VECTORS, VECTORS,...  4.83 us
    pallas_call x1, Pallas kernels, pack_x(): pl.pallas_call(pack_x_kernel, out_shape=(shape, shape), in_specs=[HBM] *...  2.58 us
    pallas_call x1, Pallas kernels, outer_columns(): pl.pallas_call(outer_kernel, out_shape=(FIELD, FIELD, TOPS, jax.ShapeDtyp...  2.27 us
    pallas_call x1, Pallas kernels, pack_y(): pl.pallas_call(pack_y_kernel, out_shape=(shape, shape), in_specs=[VMEM] *...  0.55 us
  transfers between devices with their start and end apart: 4, of which 0 were waited for; matrix products, arithmetic and copies ran while one was open for 0% of the time, Pallas kernels for 39%

profile of v2, /device:TPU:1, one launch (start us, length us, event | category | flops | bytes accessed | tf_op | source)
XLA Modules:
  0.0 25.5 jit_solution(1336853342628633351)
XLA Ops:
  0.0 2.6 %pack_x.1 = (f32[32,2048]{1,0:T(8,128)S(1)}, f32[32,2048]{1,0:T(8,128)S(1)}) custom-call(f32[19,32,2048]{2,1,0:T(8,128)} %adjoint.3, f32[2,3,32,2048]{3,2,1,0:T(8,128)} %velocity.3, f32[2,32,2048]{2,1,0:T(8,128)} %density.3, s32[32,32]{1,0:T(8,128)} %heights_hbm.3, s32[1,1,128]{2,1,0:T(1,128)} %cells_hbm.3, f32[2,3,1,1,128]{4,3,2,1,0:T(1,128)} %misfit_hbm.3), custom_call_target="tpu_custom_call" | custom-call | tf_op jit(solution)/shard_map/pack_x/pallas_call | solution.py:281
  2.6 2.8 %collective-permute-start = (f32[32,2048]{1,0:T(8,128)S(1)}, f32[32,2048]{1,0:T(8,128)S(1)}, u32[]{:S(2)}, u32[]{:S(2)}) collective-permute-start(f32[32,2048]{1,0:T(8,128)S(1)} %get-tuple-element.26), channel_id=1, source_target_pairs={{0,112},{16,32},{32,16},{48,64},{64,48},{80,96},{96,80},{112,0},{1... | collective-permute-start | bytes 786440 | tf_op jit(solution)/shard_map/ppermute | solution.py:693
  5.4 1.3 %collective-permute-start.1 = (f32[32,2048]{1,0:T(8,128)S(1)}, f32[32,2048]{1,0:T(8,128)S(1)}, u32[]{:S(2)}, u32[]{:S(2)}) collective-permute-start(f32[32,2048]{1,0:T(8,128)S(1)} %get-tuple-element.27), channel_id=1, source_target_pairs={{0,16},{16,0},{32,48},{48,32},{64,80},{80,64},{96,112},{112,96},{1... | collective-permute-start | bytes 786440 | tf_op jit(solution)/shard_map/ppermute | solution.py:693
  6.6 4.8 %prepare.1 = (f32[17,19,48,128]{3,2,1,0:T(8,128)S(1)}, f32[17,19,48,128]{3,2,1,0:T(8,128)S(1)}, f32[16,2,3,48,128]{4,3,2,1,0:T(8,128)S(1)}, f32[16,2,3,48,128]{4...) custom-call(f32[19,32,2048]{2,1,0:T(8,128)} %adjoint.3, f32[2,3,32,2048]{3,2,1,0:T(8,128)} %velocity.3, ...), custom_call_target="tpu_custom_call" | custom-call | flops 40000000 | bytes 8000000 | tf_op jit(solution)/shard_map/prepare/pallas_call | solution.py:442
  11.5 0.0 collective-permute-done.msg_a
  11.5 0.0 collective-permute-done.1.msg_b
  11.5 0.5 %pack_y.1 = (f32[7,40,128]{2,1,0:T(8,128)S(1)}, f32[7,40,128]{2,1,0:T(8,128)S(1)}) custom-call(f32[48,128]{1,0:T(8,128)S(1)} %get-tuple-element.22.own_tall, f32[17,19,48,128]{3,2,1,0:T(8,128)S(1)} %get-tuple-element.23.all_field.field_in, f32[16,2,3,48,128]{4,3,2,1,0:T(8,128)S(1)} %get-tuple-element.24.all_u.u_in, ...), custom_call_target="tpu_custom_call" | custom-call | tf_op jit(solution)/shard_map/pack_y/pallas_call | solution.py:534
  12.0 6.0 %collective-permute-start.2 = (f32[7,40,128]{2,1,0:T(8,128)S(1)}, f32[7,40,128]{2,1,0:T(8,128)S(1)}, u32[]{:S(2)}, u32[]{:S(2)}) collective-permute-start(f32[7,40,128]{2,1,0:T(8,128)S(1)} %get-tuple-element.28.order), channel_id=1, source_target_pairs={{0,15},{1,2},{2,1},{3,4},{4,3},{5,6},{6,5},{7,8},{8,7},{9,10},{10,... | collective-permute-start | bytes 430088 | tf_op jit(solution)/shard_map/ppermute | solution.py:693
  18.1 0.0 collective-permute-start.3
  18.1 5.2 %inner_columns.1 = (f32[17,19,48,128]{3,2,1,0:T(8,128)S(1)}, f32[17,19,48,128]{3,2,1,0:T(8,128)S(1)}, f32[16,2,3,48,128]{4,3,2,1,0:T(8,128)S(1)}, f32[16,2,3,48,...) custom-call(f32[48,128]{1,0:T(8,128)S(1)} %get-tuple-element.22.own_, ...), custom_call_target="tpu_custom_call", output_to_operand_aliasing={{0}: (4, {}), {1}: (5, {}), {2}: (6, {}), {3}: (7, {}), {4}... | custom-call | flops 40000000 | bytes 8000000 | tf_op jit(solution)/shard_map/inner_columns/pallas_call | solution.py:598
  23.3 0.0 collective-permute-done.2.msg_a
  23.3 0.0 collective-permute-done.3.msg_b
  23.3 2.3 %outer_columns.1 = (f32[17,19,48,128]{3,2,1,0:T(8,128)S(1)}, f32[17,19,48,128]{3,2,1,0:T(8,128)S(1)}, f32[3,17,48,128]{3,2,1,0:T(8,128)S(1)}, f32[19,32,2048]{2,1,0:T(8,128)}) custom-call(f32[7,40,128]{2,1,0:T(8,128)S(1)} %collective-permute-done.2.msg_a, ...), custom_call_target="tpu_custom_call", output_to_operand_aliasing={{0}: (2, {}), {1}: (3, {}), {2}: (6, {}), {3}: (7, {})} | custom-call | tf_op jit(solution)/shard_map/outer_columns/pallas_call | solution.py:670
Async XLA Ops:
  2.6 8.9 %collective-permute-start = (f32[32,2048]{1,0:T(8,128)S(1)}, f32[32,2048]{1,0:T(8,128)S(1)}, u32[]{:S(2)}, u32[]{:S(2)}) collective-permute-start(f32[32,2048]{1,0:T(8,128)S(1)} %get-tuple-element.26), channel_id=1, source_target_pairs={{0,112},{16,32},{32,16},{48,64},{64,48},{80,96},{96,80},{112,0},{1... | collective-permute-start | bytes 786440 | tf_op jit(solution)/shard_map/ppermute | solution.py:693
  5.4 6.1 %collective-permute-start.1 = (f32[32,2048]{1,0:T(8,128)S(1)}, f32[32,2048]{1,0:T(8,128)S(1)}, u32[]{:S(2)}, u32[]{:S(2)}) collective-permute-start(f32[32,2048]{1,0:T(8,128)S(1)} %get-tuple-element.27), channel_id=1, source_target_pairs={{0,16},{16,0},{32,48},{48,32},{64,80},{80,64},{96,112},{112,96},{1... | collective-permute-start | bytes 786440 | tf_op jit(solution)/shard_map/ppermute | solution.py:693
  12.0 11.2 %collective-permute-start.2 = (f32[7,40,128]{2,1,0:T(8,128)S(1)}, f32[7,40,128]{2,1,0:T(8,128)S(1)}, u32[]{:S(2)}, u32[]{:S(2)}) collective-permute-start(f32[7,40,128]{2,1,0:T(8,128)S(1)} %get-tuple-element.28.order), channel_id=1, source_target_pairs={{0,15},{1,2},{2,1},{3,4},{4,3},{5,6},{6,5},{7,8},{8,7},{9,10},{10,... | collective-permute-start | bytes 430088 | tf_op jit(solution)/shard_map/ppermute | solution.py:693
  18.1 5.2 %collective-permute-start.3 = (f32[7,40,128]{2,1,0:T(8,128)S(1)}, f32[7,40,128]{2,1,0:T(8,128)S(1)}, u32[]{:S(2)}, u32[]{:S(2)}) collective-permute-start(f32[7,40,128]{2,1,0:T(8,128)S(1)} %get-tuple-element.29), channel_id=1, source_target_pairs={{0,1},{1,0},{2,3},{3,2},{4,5},{5,4},{6,7},{7,6},{8,9},{9,8},{10,11... | collective-permute-start | bytes 430088 | tf_op jit(solution)/shard_map/ppermute | solution.py:693

commit v3 on v2

--- a/solution.py
+++ b/solution.py
@@ -273,7 +273,7 @@
         pack("lo", out_a)
         pack("hi", out_b)
 
-    by_parity(lax.axis_index("gx") % 2, upper, lower)
+    by_parity(1 - lax.axis_index("gx") % 2, upper, lower)
 
 
 def pack_x(adjoint, velocity, density, heights, cells, misfit):
@@ -358,6 +358,7 @@
 
 
 WIDE = TILES + 1
+SENT_EARLY = 10
 FIELD = jax.ShapeDtypeStruct((WIDE, K, EXT, 128), F32)
 VECTORS = jax.ShapeDtypeStruct((TILES, 2, 3, EXT, 128), F32)
 TOPS = jax.ShapeDtypeStruct((3, WIDE, EXT, 128), F32)
@@ -474,7 +475,7 @@
             for slot, tile in slots:
                 place_x(message, side, slot, tile, field, u, force)
 
-    by_parity(lax.axis_index("gx") % 2, lambda: from_x(msg_a, msg_b), lambda: from_x(msg_b, msg_a))
+    by_parity(1 - lax.axis_index("gx") % 2, lambda: from_x(msg_a, msg_b), lambda: from_x(msg_b, msg_a))
     for slot, tile in slots:
         for row in range(0, EXT, 8):
             value = column_tops(tall, tile, row)
@@ -566,7 +567,7 @@
             for tile in range(TILES):
                 place_x(message, side, tile, tile, field, u, force)
 
-    by_parity(lax.axis_index("gx") % 2, lambda: from_x(msg_a, msg_b), lambda: from_x(msg_b, msg_a))
+    by_parity(1 - lax.axis_index("gx") % 2, lambda: from_x(msg_a, msg_b), lambda: from_x(msg_b, msg_a))
     for tile in range(TILES):
         for row in (0, BASE + ROWS):
             tops[0, tile, row : row + 8] = column_tops(tall, tile, row)
@@ -583,7 +584,7 @@
     def second(tile, carry):
         edges(tile + 1)
         step(geo, 0, middle, field, u, force, tops, STARTS_OWN, tile, tile + 1, tile - 1)
-        send_out(field, out, sems, tile).start()
+        pl.when(tile < SENT_EARLY)(lambda: send_out(field, out, sems, tile).start())
         return carry
 
     def sent(tile, carry):
@@ -591,7 +592,7 @@
         return carry
 
     lax.fori_loop(2, TILES - 2, second, 0)
-    lax.fori_loop(2, TILES - 2, sent, 0)
+    lax.fori_loop(2, SENT_EARLY, sent, 0)
 
 
 def inner_columns(heights, msg_a, msg_b, order, field, middle, u, force, tops, shape):
@@ -611,6 +612,8 @@
 def outer_kernel(msg_a, msg_b, field_in, middle_in, u, force, tops_in, out_in,
                  field, middle, tops, out, side_partial, side_u, sems):
     del field_in, middle_in, tops_in, out_in
+    for tile in range(SENT_EARLY, TILES - 2):
+        send_out(field, out, sems, tile).start()
     geo = Geometry()
 
     def from_y(low_msg, high_msg):
@@ -662,7 +665,7 @@
         before = TILES if tile == 0 else tile - 1
         step(geo, 0, middle, field, u, force, tops, STARTS_OWN, tile, tile + 1, before)
         send_out(field, out, sems, tile).start()
-    for tile in last:
+    for tile in tuple(range(SENT_EARLY, TILES - 2)) + last:
         send_out(field, out, sems, tile).wait()
 
 
@@ -699,7 +702,7 @@
         for value in (adjoint, velocity, density, heights, cells, misfit)
     ]
     x_a, x_b = pack_x(*args)
-    x_a, x_b = swap(x_a, "gx", True), swap(x_b, "gx", False)
+    x_a, x_b = swap(x_a, "gx", False), swap(x_b, "gx", True)
     field, middle, u, force, tops, tall = prepare(*args)
     own_a, own_b = pack_y(tall, field, u, force, x_a, x_b)
     y_a, y_b = swap(own_a, "gy", True), swap(own_b, "gy", False)

time: 25.8 us -> 25.2 us (0.977)
  the two profiles are of different devices: /device:TPU:1 before, /device:TPU:0 now
where the time goes in v3:
time: 25.2 us; the launch traced here: 25 us
  Pallas kernels  14.8 us (59%)
  starting transfers between devices  9.6 us (38%)
  waiting for transfers between devices  0.48 us (2%)
    ppermute x4, starting transfers between devices, swap(): return lax.ppermute(value, axis, partners(lax.axis_size(axis), odd))  9.6 us
    pallas_call x1, Pallas kernels, prepare(): pl.pallas_call(prepare_kernel, out_shape=(FIELD, FIELD, VECTORS, VECTORS,...  4.83 us
    pallas_call x1, Pallas kernels, inner_columns(): pl.pallas_call(inner_kernel, out_shape=(FIELD, FIELD, VECTORS, VECTORS, T...  4.61 us
    pallas_call x1, Pallas kernels, pack_x(): pl.pallas_call(pack_x_kernel, out_shape=(shape, shape), in_specs=[HBM] *...  2.58 us
    pallas_call x1, Pallas kernels, outer_columns(): pl.pallas_call(outer_kernel, out_shape=(FIELD, FIELD, TOPS, jax.ShapeDtyp...  2.25 us
    pallas_call x1, Pallas kernels, pack_y(): pl.pallas_call(pack_y_kernel, out_shape=(shape, shape), in_specs=[VMEM] *...  0.55 us
  transfers between devices with their start and end apart: 4, of which 1 were waited for; matrix products, arithmetic and copies ran while one was open for 0% of the time, Pallas kernels for 38%

profile of v3, /device:TPU:0, one launch (start us, length us, event | category | flops | bytes accessed | tf_op | source)
XLA Modules:
  0.0 25.0 jit_solution(8360211812650330615)
XLA Ops:
  0.0 2.6 %pack_x.1 = (f32[32,2048]{1,0:T(8,128)S(1)}, f32[32,2048]{1,0:T(8,128)S(1)}) custom-call(f32[19,32,2048]{2,1,0:T(8,128)} %adjoint.3, f32[2,3,32,2048]{3,2,1,0:T(8,128)} %velocity.3, f32[2,32,2048]{2,1,0:T(8,128)} %density.3, s32[32,32]{1,0:T(8,128)} %heights_hbm.3, s32[1,1,128]{2,1,0:T(1,128)} %cells_hbm.3, f32[2,3,1,1,128]{4,3,2,1,0:T(1,128)} %misfit_hbm.3), custom_call_target="tpu_custom_call" | custom-call | tf_op jit(solution)/shard_map/pack_x/pallas_call | solution.py:281
  2.6 0.1 collective-permute-start
  2.7 3.2 %collective-permute-start.1 = (f32[32,2048]{1,0:T(8,128)S(1)}, f32[32,2048]{1,0:T(8,128)S(1)}, u32[]{:S(2)}, u32[]{:S(2)}) collective-permute-start(f32[32,2048]{1,0:T(8,128)S(1)} %get-tuple-element.27), channel_id=1, source_target_pairs={{0,112},{16,32},{32,16},{48,64},{64,48},{80,96},{96,80},{112,0},{1... | collective-permute-start | bytes 786440 | tf_op jit(solution)/shard_map/ppermute | solution.py:696
  5.9 4.8 %prepare.1 = (f32[17,19,48,128]{3,2,1,0:T(8,128)S(1)}, f32[17,19,48,128]{3,2,1,0:T(8,128)S(1)}, f32[16,2,3,48,128]{4,3,2,1,0:T(8,128)S(1)}, f32[16,2,3,48,128]{4...) custom-call(f32[19,32,2048]{2,1,0:T(8,128)} %adjoint.3, f32[2,3,32,2048]{3,2,1,0:T(8,128)} %velocity.3, ...), custom_call_target="tpu_custom_call" | custom-call | flops 40000000 | bytes 8000000 | tf_op jit(solution)/shard_map/prepare/pallas_call | solution.py:443
  10.7 0.0 collective-permute-done.msg_a
  10.7 0.0 collective-permute-done.1.msg_b
  10.7 0.5 %pack_y.1 = (f32[7,40,128]{2,1,0:T(8,128)S(1)}, f32[7,40,128]{2,1,0:T(8,128)S(1)}) custom-call(f32[48,128]{1,0:T(8,128)S(1)} %get-tuple-element.22.own_tall, f32[17,19,48,128]{3,2,1,0:T(8,128)S(1)} %get-tuple-element.23.all_field.field_in, f32[16,2,3,48,128]{4,3,2,1,0:T(8,128)S(1)} %get-tuple-element.24.all_u.u_in, ...), custom_call_target="tpu_custom_call" | custom-call | tf_op jit(solution)/shard_map/pack_y/pallas_call | solution.py:535
  11.3 6.3 %collective-permute-start.2 = (f32[7,40,128]{2,1,0:T(8,128)S(1)}, f32[7,40,128]{2,1,0:T(8,128)S(1)}, u32[]{:S(2)}, u32[]{:S(2)}) collective-permute-start(f32[7,40,128]{2,1,0:T(8,128)S(1)} %get-tuple-element.28.order), channel_id=1, source_target_pairs={{0,15},{1,2},{2,1},{3,4},{4,3},{5,6},{6,5},{7,8},{8,7},{9,10},{10,... | collective-permute-start | bytes 430088 | tf_op jit(solution)/shard_map/ppermute | solution.py:696
  17.6 0.0 collective-permute-start.3
  17.6 4.6 %inner_columns.1 = (f32[17,19,48,128]{3,2,1,0:T(8,128)S(1)}, f32[17,19,48,128]{3,2,1,0:T(8,128)S(1)}, f32[16,2,3,48,128]{4,3,2,1,0:T(8,128)S(1)}, f32[16,2,3,48,...) custom-call(f32[48,128]{1,0:T(8,128)S(1)} %get-tuple-element.22.own_, ...), custom_call_target="tpu_custom_call", output_to_operand_aliasing={{0}: (4, {}), {1}: (5, {}), {2}: (6, {}), {3}: (7, {}), {4}... | custom-call | flops 40000000 | bytes 8000000 | tf_op jit(solution)/shard_map/inner_columns/pallas_call | solution.py:599
  22.2 0.0 collective-permute-done.2.msg_a
  22.2 0.5 %collective-permute-done.3.msg_b = f32[7,40,128]{2,1,0:T(8,128)S(1)} collective-permute-done((f32[7,40,128]{2,1,0:T(8,128)S(1)}, f32[7,40,128]{2,1,0:T(8,128)S(1)}, u32[]{:S(2)}, u32[]{:S(2)}) %collective-permute-start.3) | collective-permute-done | bytes 143392 | tf_op jit(solution)/shard_map/ppermute | solution.py:696
  22.7 2.3 %outer_columns.1 = (f32[17,19,48,128]{3,2,1,0:T(8,128)S(1)}, f32[17,19,48,128]{3,2,1,0:T(8,128)S(1)}, f32[3,17,48,128]{3,2,1,0:T(8,128)S(1)}, f32[19,32,2048]{2,1,0:T(8,128)}) custom-call(f32[7,40,128]{2,1,0:T(8,128)S(1)} %collective-permute-done.2.msg_a, ...), custom_call_target="tpu_custom_call", output_to_operand_aliasing={{0}: (2, {}), {1}: (3, {}), {2}: (6, {}), {3}: (7, {})} | custom-call | tf_op jit(solution)/shard_map/outer_columns/pallas_call | solution.py:673
Async XLA Ops:
  2.6 8.1 %collective-permute-start = (f32[32,2048]{1,0:T(8,128)S(1)}, f32[32,2048]{1,0:T(8,128)S(1)}, u32[]{:S(2)}, u32[]{:S(2)}) collective-permute-start(f32[32,2048]{1,0:T(8,128)S(1)} %get-tuple-element.26), channel_id=1, source_target_pairs={{0,16},{16,0},{32,48},{48,32},{64,80},{80,64},{96,112},{112,96},{1... | collective-permute-start | bytes 786440 | tf_op jit(solution)/shard_map/ppermute | solution.py:696
  2.7 8.1 %collective-permute-start.1 = (f32[32,2048]{1,0:T(8,128)S(1)}, f32[32,2048]{1,0:T(8,128)S(1)}, u32[]{:S(2)}, u32[]{:S(2)}) collective-permute-start(f32[32,2048]{1,0:T(8,128)S(1)} %get-tuple-element.27), channel_id=1, source_target_pairs={{0,112},{16,32},{32,16},{48,64},{64,48},{80,96},{96,80},{112,0},{1... | collective-permute-start | bytes 786440 | tf_op jit(solution)/shard_map/ppermute | solution.py:696
  11.3 10.9 %collective-permute-start.2 = (f32[7,40,128]{2,1,0:T(8,128)S(1)}, f32[7,40,128]{2,1,0:T(8,128)S(1)}, u32[]{:S(2)}, u32[]{:S(2)}) collective-permute-start(f32[7,40,128]{2,1,0:T(8,128)S(1)} %get-tuple-element.28.order), channel_id=1, source_target_pairs={{0,15},{1,2},{2,1},{3,4},{4,3},{5,6},{6,5},{7,8},{8,7},{9,10},{10,... | collective-permute-start | bytes 430088 | tf_op jit(solution)/shard_map/ppermute | solution.py:696
  17.6 5.1 %collective-permute-start.3 = (f32[7,40,128]{2,1,0:T(8,128)S(1)}, f32[7,40,128]{2,1,0:T(8,128)S(1)}, u32[]{:S(2)}, u32[]{:S(2)}) collective-permute-start(f32[7,40,128]{2,1,0:T(8,128)S(1)} %get-tuple-element.29), channel_id=1, source_target_pairs={{0,1},{1,0},{2,3},{3,2},{4,5},{5,4},{6,7},{7,6},{8,9},{9,8},{10,11... | collective-permute-start | bytes 430088 | tf_op jit(solution)/shard_map/ppermute | solution.py:696

commit v4 on v3

--- a/solution.py
+++ b/solution.py
@@ -37,7 +37,7 @@
 SENS = 128
 STARTS_WIDE = (7, 15, 23, 31, 33)
 STARTS_OWN = (8, 16, 24, 32)
-STARTS_INNER = (9, 17, 25, 31)
+STARTS_INNER = (9, 17, 25)
 STARTS_EDGE = (7, 33)
 X_SIDE = {"lo": (1, 7, 9, 11, 13), "hi": (2, 8, 10, 12, 14)}
 Y_SIDE = {"lo": (3, 7, 10, 15, 17), "hi": (4, 8, 9, 16, 18)}

time: 25.2 us -> 24.9 us (0.988)
  Pallas kernels: 14.8 us -> 14.4 us
    pallas_call x1, Pallas kernels: 4.83 us -> 4.45 us  [prepare(): pl.pallas_call(prepare_kernel, out_shape=(FIELD, FIELD, VECTORS, VECTORS,...]
  transfers between devices with their start and end apart: 4 -> 4, of which waited for: 1 -> 1; matrix products, arithmetic and copies ran while one was open for 0% -> 0% of each run, Pallas kernels for 38% -> 37%
where the time goes in v4:
time: 24.9 us; the launch traced here: 24.6 us
  Pallas kernels  14.4 us (58%)
  starting transfers between devices  9.6 us (39%)
  waiting for transfers between devices  0.48 us (2%)
    ppermute x4, starting transfers between devices, swap(): return lax.ppermute(value, axis, partners(lax.axis_size(axis), odd))  9.6 us
    pallas_call x1, Pallas kernels, inner_columns(): pl.pallas_call(inner_kernel, out_shape=(FIELD, FIELD, VECTORS, VECTORS, T...  4.61 us
    pallas_call x1, Pallas kernels, prepare(): pl.pallas_call(prepare_kernel, out_shape=(FIELD, FIELD, VECTORS, VECTORS,...  4.45 us
    pallas_call x1, Pallas kernels, pack_x(): pl.pallas_call(pack_x_kernel, out_shape=(shape, shape), in_specs=[HBM] *...  2.58 us
    pallas_call x1, Pallas kernels, outer_columns(): pl.pallas_call(outer_kernel, out_shape=(FIELD, FIELD, TOPS, jax.ShapeDtyp...  2.25 us
    pallas_call x1, Pallas kernels, pack_y(): pl.pallas_call(pack_y_kernel, out_shape=(shape, shape), in_specs=[VMEM] *...  0.55 us
  transfers between devices with their start and end apart: 4, of which 1 were waited for; matrix products, arithmetic and copies ran while one was open for 0% of the time, Pallas kernels for 37%

profile of v4, /device:TPU:0, one launch (start us, length us, event | category | flops | bytes accessed | tf_op | source)
XLA Modules:
  0.0 24.6 jit_solution(15515836246143626870)
XLA Ops:
  0.0 2.6 %pack_x.1 = (f32[32,2048]{1,0:T(8,128)S(1)}, f32[32,2048]{1,0:T(8,128)S(1)}) custom-call(f32[19,32,2048]{2,1,0:T(8,128)} %adjoint.3, f32[2,3,32,2048]{3,2,1,0:T(8,128)} %velocity.3, f32[2,32,2048]{2,1,0:T(8,128)} %density.3, s32[32,32]{1,0:T(8,128)} %heights_hbm.3, s32[1,1,128]{2,1,0:T(1,128)} %cells_hbm.3, f32[2,3,1,1,128]{4,3,2,1,0:T(1,128)} %misfit_hbm.3), custom_call_target="tpu_custom_call" | custom-call | tf_op jit(solution)/shard_map/pack_x/pallas_call | solution.py:281
  2.6 0.1 collective-permute-start
  2.7 3.2 %collective-permute-start.1 = (f32[32,2048]{1,0:T(8,128)S(1)}, f32[32,2048]{1,0:T(8,128)S(1)}, u32[]{:S(2)}, u32[]{:S(2)}) collective-permute-start(f32[32,2048]{1,0:T(8,128)S(1)} %get-tuple-element.27), channel_id=1, source_target_pairs={{0,112},{16,32},{32,16},{48,64},{64,48},{80,96},{96,80},{112,0},{1... | collective-permute-start | bytes 786440 | tf_op jit(solution)/shard_map/ppermute | solution.py:696
  5.9 4.5 %prepare.1 = (f32[17,19,48,128]{3,2,1,0:T(8,128)S(1)}, f32[17,19,48,128]{3,2,1,0:T(8,128)S(1)}, f32[16,2,3,48,128]{4,3,2,1,0:T(8,128)S(1)}, f32[16,2,3,48,128]{4...) custom-call(f32[19,32,2048]{2,1,0:T(8,128)} %adjoint.3, f32[2,3,32,2048]{3,2,1,0:T(8,128)} %velocity.3, ...), custom_call_target="tpu_custom_call" | custom-call | flops 40000000 | bytes 8000000 | tf_op jit(solution)/shard_map/prepare/pallas_call | solution.py:443
  10.3 0.0 collective-permute-done.msg_a
  10.4 0.0 collective-permute-done.1.msg_b
  10.4 0.5 %pack_y.1 = (f32[7,40,128]{2,1,0:T(8,128)S(1)}, f32[7,40,128]{2,1,0:T(8,128)S(1)}) custom-call(f32[48,128]{1,0:T(8,128)S(1)} %get-tuple-element.22.own_tall, f32[17,19,48,128]{3,2,1,0:T(8,128)S(1)} %get-tuple-element.23.all_field.field_in, f32[16,2,3,48,128]{4,3,2,1,0:T(8,128)S(1)} %get-tuple-element.24.all_u.u_in, ...), custom_call_target="tpu_custom_call" | custom-call | tf_op jit(solution)/shard_map/pack_y/pallas_call | solution.py:535
  10.9 6.3 %collective-permute-start.2 = (f32[7,40,128]{2,1,0:T(8,128)S(1)}, f32[7,40,128]{2,1,0:T(8,128)S(1)}, u32[]{:S(2)}, u32[]{:S(2)}) collective-permute-start(f32[7,40,128]{2,1,0:T(8,128)S(1)} %get-tuple-element.28.order), channel_id=1, source_target_pairs={{0,15},{1,2},{2,1},{3,4},{4,3},{5,6},{6,5},{7,8},{8,7},{9,10},{10,... | collective-permute-start | bytes 430088 | tf_op jit(solution)/shard_map/ppermute | solution.py:696
  17.2 0.0 collective-permute-start.3
  17.2 4.6 %inner_columns.1 = (f32[17,19,48,128]{3,2,1,0:T(8,128)S(1)}, f32[17,19,48,128]{3,2,1,0:T(8,128)S(1)}, f32[16,2,3,48,128]{4,3,2,1,0:T(8,128)S(1)}, f32[16,2,3,48,...) custom-call(f32[48,128]{1,0:T(8,128)S(1)} %get-tuple-element.22.own_, ...), custom_call_target="tpu_custom_call", output_to_operand_aliasing={{0}: (4, {}), {1}: (5, {}), {2}: (6, {}), {3}: (7, {}), {4}... | custom-call | flops 40000000 | bytes 8000000 | tf_op jit(solution)/shard_map/inner_columns/pallas_call | solution.py:599
  21.9 0.0 collective-permute-done.2.msg_a
  21.9 0.5 %collective-permute-done.3.msg_b = f32[7,40,128]{2,1,0:T(8,128)S(1)} collective-permute-done((f32[7,40,128]{2,1,0:T(8,128)S(1)}, f32[7,40,128]{2,1,0:T(8,128)S(1)}, u32[]{:S(2)}, u32[]{:S(2)}) %collective-permute-start.3) | collective-permute-done | bytes 143392 | tf_op jit(solution)/shard_map/ppermute | solution.py:696
  22.3 2.3 %outer_columns.1 = (f32[17,19,48,128]{3,2,1,0:T(8,128)S(1)}, f32[17,19,48,128]{3,2,1,0:T(8,128)S(1)}, f32[3,17,48,128]{3,2,1,0:T(8,128)S(1)}, f32[19,32,2048]{2,1,0:T(8,128)}) custom-call(f32[7,40,128]{2,1,0:T(8,128)S(1)} %collective-permute-done.2.msg_a, ...), custom_call_target="tpu_custom_call", output_to_operand_aliasing={{0}: (2, {}), {1}: (3, {}), {2}: (6, {}), {3}: (7, {})} | custom-call | tf_op jit(solution)/shard_map/outer_columns/pallas_call | solution.py:673
Async XLA Ops:
  2.6 7.8 %collective-permute-start = (f32[32,2048]{1,0:T(8,128)S(1)}, f32[32,2048]{1,0:T(8,128)S(1)}, u32[]{:S(2)}, u32[]{:S(2)}) collective-permute-start(f32[32,2048]{1,0:T(8,128)S(1)} %get-tuple-element.26), channel_id=1, source_target_pairs={{0,16},{16,0},{32,48},{48,32},{64,80},{80,64},{96,112},{112,96},{1... | collective-permute-start | bytes 786440 | tf_op jit(solution)/shard_map/ppermute | solution.py:696
  2.7 7.7 %collective-permute-start.1 = (f32[32,2048]{1,0:T(8,128)S(1)}, f32[32,2048]{1,0:T(8,128)S(1)}, u32[]{:S(2)}, u32[]{:S(2)}) collective-permute-start(f32[32,2048]{1,0:T(8,128)S(1)} %get-tuple-element.27), channel_id=1, source_target_pairs={{0,112},{16,32},{32,16},{48,64},{64,48},{80,96},{96,80},{112,0},{1... | collective-permute-start | bytes 786440 | tf_op jit(solution)/shard_map/ppermute | solution.py:696
  10.9 10.9 %collective-permute-start.2 = (f32[7,40,128]{2,1,0:T(8,128)S(1)}, f32[7,40,128]{2,1,0:T(8,128)S(1)}, u32[]{:S(2)}, u32[]{:S(2)}) collective-permute-start(f32[7,40,128]{2,1,0:T(8,128)S(1)} %get-tuple-element.28.order), channel_id=1, source_target_pairs={{0,15},{1,2},{2,1},{3,4},{4,3},{5,6},{6,5},{7,8},{8,7},{9,10},{10,... | collective-permute-start | bytes 430088 | tf_op jit(solution)/shard_map/ppermute | solution.py:696
  17.2 5.1 %collective-permute-start.3 = (f32[7,40,128]{2,1,0:T(8,128)S(1)}, f32[7,40,128]{2,1,0:T(8,128)S(1)}, u32[]{:S(2)}, u32[]{:S(2)}) collective-permute-start(f32[7,40,128]{2,1,0:T(8,128)S(1)} %get-tuple-element.29), channel_id=1, source_target_pairs={{0,1},{1,0},{2,3},{3,2},{4,5},{5,4},{6,7},{7,6},{8,9},{9,8},{10,11... | collective-permute-start | bytes 430088 | tf_op jit(solution)/shard_map/ppermute | solution.py:696
